TPU v7x, 512 devices: a whole 4x4x16 slice. The times are simulated.
512 devices in a mesh: row: 16 (over x, y), col: 16 (over z_lo, core), fiber: 2 (over z_hi).
Axes of the slice: x: 4, y: 4, z: 16 (z_hi: 2, z_lo: 8; z = z_hi * 8 + z_lo), core: 2. Of those that a mesh axis runs over, the one named last changes fastest.
Arguments:
- a_blocks: bfloat16 [64, 7, 128, 128], P(('row', 'fiber')), may hold values from -0.1875 to 0.1875
- p_terms: bfloat16 [64, 7, 128, 128], P(('row', 'fiber')), may hold values from -0.1875 to 0.1875
- block_columns: int32 [64, 7], replicated, may hold values from 0 to 63, as said below
- aggregates: int32 [64], replicated, may hold values from 0 to 15
Outputs:
- coarse: float32 [2048, 2048], P('row', 'col')
Inputs may be any that keep to these rules, and one draw needn't show every extreme that they name: `block_columns`: each row names 7 distinct block columns, its own block row among them.
All inputs are finite; a program needn't handle non-finite values.
Results may differ from a plain program's by a relative error of at most 0.0003.
Values may be sent and summed in bfloat16 or wider, within the bound.
No kernel may reach another device: no remote copies, remote signals or barrier semaphores. Data moves between devices by JAX's collectives and lax.ppermute only.
A program may use at most 64 MiB of HBM per device.

v0:
```python
import jax
import jax.numpy as jnp
from jax import lax
from jax.sharding import PartitionSpec as P

CB_DEV = 1


def from_root(value, axis, source):
    kept = jnp.where(lax.axis_index(axis) == source, value, 0).astype(value.dtype)
    return lax.psum(kept, axis)


def local(a_blocks, p_terms, block_columns, aggregates):
    nfiber = lax.axis_size("fiber")
    nrow = lax.axis_size("row")
    row_id = lax.axis_index("row")
    col_id = lax.axis_index("col")
    fiber_id = lax.axis_index("fiber")
    rows_here = a_blocks.shape[0]
    slots = a_blocks.shape[1]
    blk = a_blocks.shape[2]
    fine_total = block_columns.shape[0]
    coarse_here = CB_DEV
    coarse_total = coarse_here * nrow
    fine_ids = jnp.arange(fine_total, dtype=jnp.int32)
    coarse_ids = jnp.arange(coarse_total, dtype=jnp.int32)
    hits = block_columns[:, :, None] == fine_ids[None, None, :]
    groups = jnp.sum(jnp.where(hits, aggregates[None, None, :], 0), axis=2)
    own_start = (row_id * nfiber + fiber_id) * rows_here
    own_cols = lax.dynamic_slice_in_dim(block_columns, own_start, rows_here, 0)
    own_groups = lax.dynamic_slice_in_dim(groups, own_start, rows_here, 0)
    terms_wide = p_terms.astype(jnp.float32)
    panel_terms = from_root(p_terms, "row", col_id)
    layers = lax.all_gather(panel_terms, "fiber", axis=0, tiled=True)
    panel_rows = layers.shape[0]
    panel_start = col_id * panel_rows
    panel_groups = lax.dynamic_slice_in_dim(groups, panel_start, panel_rows, 0)
    partial_value = jnp.zeros((rows_here, blk, coarse_total, blk), jnp.float32)
    for slot in range(slots):
        local_rows = own_cols[:, slot] - panel_start
        inside = (local_rows >= 0) & (local_rows < panel_rows)
        safe_rows = jnp.clip(local_rows, 0, panel_rows - 1)
        picked = jnp.take(layers, safe_rows, axis=0)
        picked_groups = jnp.take(panel_groups, safe_rows, axis=0)
        a_slot = a_blocks[:, slot] * inside[:, None, None].astype(jnp.bfloat16)
        products = jnp.einsum("ixz,iqzy->iqxy", a_slot, picked, preferred_element_type=jnp.float32)
        placing = (picked_groups[:, :, None] == coarse_ids[None, None, :]).astype(jnp.float32)
        partial_value = partial_value + jnp.einsum(
            "iqa,iqxy->ixay", placing, products, precision=lax.Precision.HIGHEST
        )
    y_panel = lax.psum_scatter(partial_value, "col", scatter_dimension=2, tiled=True)
    y_rows = y_panel.reshape(rows_here, blk, coarse_here * blk)
    own_onehot = (own_groups[:, :, None] == coarse_ids[None, None, :]).astype(jnp.float32)
    lifted = jnp.einsum("ikxc,ixb->ikcb", terms_wide, y_rows, precision=lax.Precision.HIGHEST)
    coarse_part = jnp.einsum("ika,ikcb->acb", own_onehot, lifted, precision=lax.Precision.HIGHEST)
    tile = lax.psum_scatter(coarse_part, "row", scatter_dimension=0, tiled=True)
    total = lax.psum(tile, "fiber")
    return total.reshape(coarse_here * blk, coarse_here * blk)


def solution(mesh):
    in_specs = (
        P(("row", "fiber"), None, None, None),
        P(("row", "fiber"), None, None, None),
        P(),
        P(),
    )
    out_specs = P("row", "col")
    return jax.shard_map(local, mesh=mesh, in_specs=in_specs, out_specs=out_specs, check_vma=False)
```

profile of v0, /device:TPU:1, one launch (start us, length us, event | category | flops | bytes accessed | tf_op | source)
XLA Modules:
  0.0 473.2 jit_solution(17046459853160671274)
XLA Ops:
  13.9 115.9 %all-reduce.4.cloned.1.call-done = bf16[2,7,128,128]{3,2,1,0:T(8,128)(2,1)} async-done(((bf16[2,7,128,128]{3,2,1,0:T(8,128)(2,1)}), bf16[2,7,128,128]{3,2,1,0:T(8,128)(2,1)}) %all-reduce.4.cloned.1.call-update) | async-done | bytes 458768 | tf_op jit(solution)/shard_map/psum | solution.py:11
  129.8 26.9 %all_gather.3 = bf16[4,7,128,128]{3,2,1,0:T(8,128)(2,1)S(1)} all-gather(bf16[2,7,128,128]{3,2,1,0:T(8,128)(2,1)} %all-reduce.4.cloned.1.call-done), channel_id=1, replica_groups=mesh['row'=16,'col'=16,'fiber'=2] {'fiber'}, dimensions={0}, use_global_device_ids=true | all-gather | bytes 1376256 | tf_op jit(solution)/shard_map/all_gather | solution.py:35
  157.3 1.4 gather_fusion.4
  158.7 1.4 gather_fusion.6
  160.0 1.4 gather_fusion.8
  161.4 1.4 gather_fusion
  162.8 1.4 gather_fusion.10
  164.8 1.2 convolution_bitcast_fusion.7
  166.5 1.4 convolution_bitcast_fusion.6
  168.3 1.4 convolution_bitcast_fusion.5
  169.7 1.3 copy.18
  171.0 1.4 convolution_bitcast_fusion.4
  172.5 1.4 copy.20
  173.8 1.4 convolution_bitcast_fusion.8
  175.3 1.3 copy.12
  176.6 1.4 convolution_bitcast_fusion.3
  178.0 1.3 copy.22
  179.3 2.2 convolution_bitcast_fusion.2
  181.5 1.6 copy.24
  183.1 1.1 fusion.49
  184.2 1.1 fusion.52
  185.4 1.1 fusion.55
  186.6 1.1 fusion.58
  187.9 1.1 fusion.46
  190.2 1.7 add_bitcast_fusion
  191.9 2.0 copy.25
  194.1 121.4 %reduce-scatter.5.cloned.1.call-done = f32[2,128,1,128]{3,1,0,2:T(8,128)} async-done(((f32[2,128,16,128]{3,1,0,2:T(8,128)}), f32[2,128,1,128]{3,1,0,2:T(8,128)}) %reduce-scatter.5.cloned.1.call-update) | async-done | bytes 131088 | tf_op jit(solution)/shard_map/reduce_scatter | solution.py:52
  315.5 1.5 convolution_bitcast_fusion.1
  318.3 1.3 copy.28
  319.7 88.0 %reduce-scatter.7.cloned.1.call-done = f32[1,128,128]{2,1,0:T(8,128)} async-done(((f32[16,128,128]{2,1,0:T(8,128)}), f32[1,128,128]{2,1,0:T(8,128)}) %reduce-scatter.7.cloned.1.call-update) | async-done | bytes 65552
  407.7 57.5 %all-reduce.6.cloned.1.call-done = f32[128,128]{1,0:T(8,128)} async-done(((f32[128,128]{1,0:T(8,128)}), f32[128,128]{1,0:T(8,128)}) %all-reduce.6.cloned.1.call-update) | async-done | bytes 65552 | tf_op jit(solution)/shard_map/psum | solution.py:58
  465.2 1.5 copy.57
  (52 shorter events, 12.5 us)
Async XLA Ops:
  6.5 123.2 %all-reduce.4.cloned.1.call-start = ((), (), s32[]{:S(2)}) async-start(), calls=%async_computation.2 | async-start | bytes 917504 | tf_op jit(solution)/shard_map/psum | solution.py:11
  7.4 308.2 %reduce-scatter.5.cloned.1.call-start = ((), (), s32[]{:S(2)}) async-start(), calls=%async_computation.3 | async-start | bytes 2228224 | tf_op jit(solution)/shard_map/reduce_scatter | solution.py:52
  184.2 1.2 copy-start
  185.4 1.2 copy-start.1
  186.6 1.2 copy-start.2
  187.9 1.2 copy-start.3
  193.9 121.6 %copy-start.4 = (bf16[2,7,128,128]{3,2,1,0:T(8,128)(2,1)S(1)}, bf16[2,7,128,128]{3,2,1,0:T(8,128)(2,1)}, u32[]{:S(2)}) copy-start(bf16[2,7,128,128]{3,2,1,0:T(8,128)(2,1)} %param.9) | copy-start | bytes 1376260
  193.9 213.7 %reduce-scatter.7.cloned.1.call-start = ((), (), s32[]{:S(2)}) async-start(), calls=%async_computation.5 | async-start | bytes 1114112
  319.6 145.6 %all-reduce.6.cloned.1.call-start = ((), (), s32[]{:S(2)}) async-start(), calls=%async_computation.4 | async-start | bytes 131072 | tf_op jit(solution)/shard_map/psum | solution.py:58
Sparse Core Ops, SparseCore 0:
  10.6 119.1 all-reduce.3
  194.0 121.4 reduce-scatter.4
  319.8 87.8 reduce-scatter.6
  410.6 54.5 all-reduce.5
where the time goes:
time: 474 us; the launch traced here: 473 us
  waiting for transfers between devices  383 us (81%)
  blocking collectives  26.9 us (6%)
  local copies, waits for them, and re-layouts  26.6 us (6%)
  matrix products  21.1 us (4%)
  between operations  13.3 us (3%)
    reduce_scatter x1, waiting for transfers between devices, local(): lax.psum_scatter(partial_value, 'col', scatter_dimension=2, tiled=True)  121 us
    psum x1, waiting for transfers between devices, from_root(): return lax.psum(kept, axis)  116 us
    unnamed x5, waiting for transfers between devices  88 us
    psum x1, waiting for transfers between devices, local(): total = lax.psum(tile, 'fiber')  57.5 us
    all_gather x1, blocking collectives, local(): layers = lax.all_gather(panel_terms, 'fiber', axis=0, tiled=True)  26.9 us
    dot_general x7, matrix products, local(): jnp.einsum('ixz,iqzy->iqxy', a_slot, picked, preferred_element_type=jnp.f...  10.5 us
  transfers between devices with their start and end apart: 4, of which 4 were waited for; matrix products, arithmetic and copies ran while one was open for 1% of the time, Pallas kernels for 0%

commit v1 on v0

v1 whole, which is shorter than its diff:
```python
import jax
import jax.numpy as jnp
from jax import lax
from jax.experimental import pallas as pl
from jax.experimental.pallas import tpu as pltpu
from jax.sharding import PartitionSpec as P

BLK = 128
HALF = 64
SCALE_ROWS = 16
TOP = 32766.0
STEPS = 64.0
F32 = jnp.float32
BF16 = jnp.bfloat16


def code(value):
    largest = jnp.max(jnp.abs(value), axis=0, keepdims=True)
    exponent = jnp.ceil(jnp.log2(jnp.maximum(largest, 2.0**-111)) * STEPS)
    steps = jnp.floor(value * (jnp.exp2(exponent * (-1.0 / STEPS)) * TOP) + 0.5)
    scale = jnp.broadcast_to(exponent, (SCALE_ROWS, value.shape[1]))
    return steps.astype(jnp.int32).astype(jnp.int16), scale.astype(jnp.int32).astype(jnp.int16)


def scale_of(codes):
    exponent = codes.astype(jnp.int32).astype(F32)[0:1]
    return jnp.exp2(exponent * (1.0 / STEPS)) * (1.0 / TOP)


def low_lanes(rows):
    return lax.broadcasted_iota(jnp.int32, (rows, BLK), 1) < HALF


def swap_halves(value):
    return pltpu.roll(value, HALF, 1)


def build_kernel(columns_ref, aggregates_ref, terms_ref, own_ref, partner_ref):
    rows, slots = terms_ref.shape[0], terms_ref.shape[1]
    nfiber = lax.axis_size("fiber")
    ncol = lax.axis_size("col")
    col = lax.axis_index("col")
    start = (lax.axis_index("row") * nfiber + lax.axis_index("fiber")) * rows
    working = lax.rem(col + ncol // 2, ncol)
    low = low_lanes(BLK)
    sums = [[], []]
    for q in range(rows):
        first = jnp.zeros((BLK, BLK), F32)
        second = jnp.zeros((BLK, BLK), F32)
        for k in range(slots):
            group = aggregates_ref[columns_ref[start + q, k]]
            term = terms_ref[q, k].astype(F32)
            first = first + term * jnp.where(group == working, 1.0, 0.0)
            second = second + term * jnp.where(group == col, 1.0, 0.0)
        sums[0].append(first)
        sums[1].append(second)
    for out_ref, (p0, p1) in zip((own_ref, partner_ref), sums):
        packed = (jnp.where(low, p0, swap_halves(p1)), jnp.where(low, swap_halves(p0), p1))
        for h in range(2):
            steps, scale = code(packed[h])
            out_ref[h, 0:BLK, :] = steps
            out_ref[h, BLK : BLK + SCALE_ROWS, :] = scale


def main_kernel(columns_ref, aggregates_ref, gathered_ref, a_own, p_own, a_pair, p_pair, out_ref, total):
    rows, slots = a_own.shape[0], a_own.shape[1]
    nfiber = lax.axis_size("fiber")
    fiber = lax.axis_index("fiber")
    row = lax.axis_index("row")
    low = low_lanes(BLK)
    lane_half = lax.broadcasted_iota(jnp.int32, (1, BLK), 1) // HALF
    total[...] = jnp.zeros_like(total)
    for a_ref, p_ref, panel in ((a_own, p_own, row), (a_pair, p_pair, row ^ 4)):
        for q in range(rows):
            i = (panel * nfiber + fiber) * rows + q
            y = jnp.zeros((BLK, 2 * BLK), F32)
            for k in range(slots):
                j = columns_ref[i, k]
                source = j // 4
                layer = (j // 2) % 2
                other = jnp.where(layer == fiber, 0, 1)
                factor = scale_of(gathered_ref[source, other, BLK : BLK + SCALE_ROWS, :])
                factor = jnp.where(lane_half == j % 2, factor, 0.0)
                block = gathered_ref[source, other, 0:BLK, :].astype(jnp.int32).astype(F32) * factor
                high = block.astype(BF16)
                rest = (block - high.astype(F32)).astype(BF16)
                y = y + jnp.dot(a_ref[q, k], jnp.concatenate([high, rest], axis=1), preferred_element_type=F32)
            y = y[:, :BLK] + y[:, BLK:]
            y = y + swap_halves(y)
            high = y.astype(BF16).astype(F32)
            split = jnp.where(low, high, y - high).astype(BF16)
            for k in range(slots):
                group = aggregates_ref[columns_ref[i, k]]
                lifted = lax.dot_general(p_ref[q, k], split, (((0,), (0,)), ((), ())), preferred_element_type=F32)
                total[group] += lifted
    low = low_lanes(HALF)
    for coarse in range(total.shape[0]):
        tile = total[coarse]
        tile = tile + swap_halves(tile)
        steps, scale = code(jnp.where(low, tile[:HALF], tile[HALF:]))
        out_ref[coarse, 0:HALF, :] = steps
        out_ref[coarse, HALF : HALF + SCALE_ROWS, :] = scale


def sum_kernel(parts_ref, out_ref):
    low = low_lanes(HALF)
    halves = [jnp.zeros((HALF, BLK), F32), jnp.zeros((HALF, BLK), F32)]
    for source in range(parts_ref.shape[0]):
        h = (source // 4) % 2
        factor = scale_of(parts_ref[source, HALF : HALF + SCALE_ROWS, :])
        halves[h] = halves[h] + parts_ref[source, 0:HALF, :].astype(jnp.int32).astype(F32) * factor
    left, right = halves
    out_ref[0:HALF, :] = jnp.where(low, left, swap_halves(right))
    out_ref[HALF:BLK, :] = jnp.where(low, swap_halves(left), right)


SMEM = pl.BlockSpec(memory_space=pltpu.SMEM)
VMEM = pl.BlockSpec(memory_space=pltpu.VMEM)


def local(a_blocks, p_terms, block_columns, aggregates):
    nrow = lax.axis_size("row")
    ncol = lax.axis_size("col")
    nfiber = lax.axis_size("fiber")
    pairs = [(r, r ^ 4) for r in range(nrow)]

    def along(step):
        moves = []
        for c in range(ncol):
            for f in range(nfiber):
                z = (f * (ncol // 2) + c // 2 + step) % ncol
                moves.append((c * nfiber + f, (z % (ncol // 2) * 2 + c % 2) * nfiber + z // (ncol // 2)))
        return moves

    across = [
        (c * nfiber + f, (c + ncol // 2) % ncol * nfiber + 1 - f) for c in range(ncol) for f in range(nfiber)
    ]
    unit = jax.ShapeDtypeStruct((2, BLK + SCALE_ROWS, BLK), jnp.int16)
    own, partner = pl.pallas_call(
        build_kernel,
        out_shape=(unit, unit),
        in_specs=[SMEM, SMEM, VMEM],
        out_specs=(VMEM, VMEM),
        name="build",
    )(block_columns, aggregates, p_terms)
    crossed = lax.ppermute(partner, ("col", "fiber"), across)
    a_pair = lax.ppermute(a_blocks, "row", pairs)
    p_pair = lax.ppermute(p_terms, "row", pairs)
    both = jnp.stack([own, crossed], axis=1)
    sent = jnp.broadcast_to(both[None, :, None], (nrow // 8, 2, 4) + both.shape[1:]).reshape((nrow,) + both.shape[1:])
    gathered = lax.all_to_all(sent, "row", 0, 0, tiled=True)
    parts = pl.pallas_call(
        main_kernel,
        out_shape=jax.ShapeDtypeStruct((nrow, HALF + SCALE_ROWS, BLK), jnp.int16),
        in_specs=[SMEM, SMEM] + [VMEM] * 5,
        out_specs=VMEM,
        scratch_shapes=[pltpu.VMEM((nrow, BLK, BLK), F32)],
        compiler_params=pltpu.CompilerParams(vmem_limit_bytes=32 * 1024 * 1024),
        name="main",
    )(block_columns, aggregates, gathered, a_blocks, p_terms, a_pair, p_pair)
    received = lax.all_to_all(parts, "row", 0, 0, tiled=True)
    tile = pl.pallas_call(
        sum_kernel,
        out_shape=jax.ShapeDtypeStruct((BLK, BLK), F32),
        in_specs=[VMEM],
        out_specs=VMEM,
        name="sum",
    )(received)
    up = lax.ppermute(tile, ("col", "fiber"), along(ncol // 4))
    down = lax.ppermute(tile, ("col", "fiber"), along(-(ncol // 4)))
    return up + down


def solution(mesh):
    in_specs = (
        P(("row", "fiber"), None, None, None),
        P(("row", "fiber"), None, None, None),
        P(),
        P(),
    )
    out_specs = P("row", "col")
    return jax.shard_map(local, mesh=mesh, in_specs=in_specs, out_specs=out_specs, check_vma=False)
```

time: 474 us -> 104 us (0.22)
  the two profiles are of different devices: /device:TPU:1 before, /device:TPU:8 now
where the time goes in v1:
time: 104 us; the launch traced here: 103 us
  waiting for transfers between devices  40.7 us (39%)
  starting transfers between devices  36.3 us (35%)
  blocking collectives  14.1 us (14%)
  Pallas kernels  7.77 us (7%)
  local copies, waits for them, and re-layouts  2.59 us (2%)
  other arithmetic  1.53 us (1%)
    ppermute x1, waiting for transfers between devices, local(): a_pair = lax.ppermute(a_blocks, 'row', pairs)  19.9 us
    all_to_all x1, blocking collectives, local(): received = lax.all_to_all(parts, 'row', 0, 0, tiled=True)  14.1 us
    ppermute x1, starting transfers between devices, local(): crossed = lax.ppermute(partner, ('col', 'fiber'), across)  12.7 us
    ppermute x1, waiting for transfers between devices, local(): p_pair = lax.ppermute(p_terms, 'row', pairs)  7.94 us
    all_to_all x1, starting transfers between devices, local(): gathered = lax.all_to_all(sent, 'row', 0, 0, tiled=True)  7.54 us
    ppermute x1, waiting for transfers between devices, local(): crossed = lax.ppermute(partner, ('col', 'fiber'), across)  6.59 us
    ppermute x1, starting transfers between devices, local(): up = lax.ppermute(tile, ('col', 'fiber'), along(ncol // 4))  6.27 us
    ppermute x1, waiting for transfers between devices, local(): down = lax.ppermute(tile, ('col', 'fiber'), along(-(ncol // 4)))  5.69 us
  transfers between devices with their start and end apart: 6, of which 5 were waited for; matrix products, arithmetic and copies ran while one was open for 0% of the time, Pallas kernels for 0%

profile of v1, /device:TPU:8, one launch (start us, length us, event | category | flops | bytes accessed | tf_op | source)
XLA Modules:
  0.0 103.2 jit_solution(4456909385676947990)
XLA Ops:
  0.0 1.4 %copy.7.columns_ref = s32[64,7]{1,0:T(8,128)} copy(s32[64,7]{0,1:T(8,128)} %param.6) | data formatting | bytes 3584 | tf_op args[2]
  1.4 2.2 %build.1 = (s16[2,144,128]{2,1,0:T(8,128)(2,1)}, s16[2,144,128]{2,1,0:T(8,128)(2,1)}) custom-call(s32[64,7]{1,0:T(8,128)} %copy.7.columns_ref, s32[64]{0:T(128)} %aggregates_ref.3, bf16[2,7,128,128]{3,2,1,0:T(8,128)(2,1)} %p_own.1), custom_call_target="tpu_custom_call" | custom-call | tf_op jit(solution)/shard_map/build/pallas_call | solution.py:139
  3.6 12.7 %collective-permute-start = (s16[2,144,128]{2,1,0:T(8,128)(2,1)}, s16[2,144,128]{2,1,0:T(8,128)(2,1)S(1)}, u32[]{:S(2)}, u32[]{:S(2)}) collective-permute-start(s16[2,144,128]{2,1,0:T(8,128)(2,1)} %get-tuple-element.8), channel_id=1, source_target_pairs={{0,17},{1,16},{2,19},{3,18},{4,21},{5,20},{6,23},{7,22},{8,25},{9,... | collective-permute-start | bytes 221192 | tf_op jit(solution)/shard_map/ppermute | solution.py:146
  16.3 6.6 %collective-permute-done = s16[2,144,128]{2,1,0:T(8,128)(2,1)S(1)} collective-permute-done((s16[2,144,128]{2,1,0:T(8,128)(2,1)}, s16[2,144,128]{2,1,0:T(8,128)(2,1)S(1)}, u32[]{:S(2)}, u32[]{:S(2)}) %collective-permute-start) | collective-permute-done | bytes 73760 | tf_op jit(solution)/shard_map/ppermute | solution.py:146
  22.9 0.9 pad_add_fusion
  23.8 1.2 %broadcast_in_dim.2 = s16[2,2,4,2,144,128]{5,4,3,2,1,0:T(8,128)(2,1)} broadcast(s16[2,2,144,128]{3,2,1,0:T(8,128)(2,1)S(1)} %copy.6), dimensions={1,3,4,5} | broadcast | bytes 1327104 | tf_op jit(solution)/shard_map/broadcast_in_dim | solution.py:150
  25.0 0.0 copy-start.1
  25.0 0.0 copy-start
  25.0 0.0 copy-start.2
  25.0 0.0 copy-start.3
  25.0 7.5 %all-to-all-start = ((s16[16,2,144,128]{3,2,1,0:T(8,128)(2,1)}), s16[16,2,144,128]{3,2,1,0:T(8,128)(2,1)S(1)}, u32[]{:S(2)}, u32[]{:S(2)}) async-start(s16[16,2,144,128]{3,2,1,0:T(8,128)(2,1)} %bitcast.2), calls=%async_computation | async-start | bytes 2359296 | tf_op jit(solution)/shard_map/all_to_all | solution.py:151
  32.5 0.0 copy-done.1
  32.5 3.4 %collective-permute-start.1 = (bf16[2,7,128,128]{3,2,1,0:T(8,128)(2,1)S(1)}, bf16[2,7,128,128]{3,2,1,0:T(8,128)(2,1)S(1)}, u32[]{:S(2)}, u32[]{:S(2)}) collective-permute-start(bf16[2,7,128,128]{3,2,1,0:T(8,128)(2,1)S(1)} %copy-done.1), channel_id=1, source_target_pairs={{0,128},{32,160},{64,192},{96,224},{128,0},{160,32},{192,64},{224,... | collective-permute-start | bytes 1376264 | tf_op jit(solution)/shard_map/ppermute | solution.py:147
  35.9 0.0 copy-done
  35.9 2.5 %collective-permute-start.2 = (bf16[2,7,128,128]{3,2,1,0:T(8,128)(2,1)S(1)}, bf16[2,7,128,128]{3,2,1,0:T(8,128)(2,1)S(1)}, u32[]{:S(2)}, u32[]{:S(2)}) collective-permute-start(bf16[2,7,128,128]{3,2,1,0:T(8,128)(2,1)S(1)} %copy-done), channel_id=1, source_target_pairs={{0,128},{32,160},{64,192},{96,224},{128,0},{160,32},{192,64},{224,... | collective-permute-start | bytes 1376264 | tf_op jit(solution)/shard_map/ppermute | solution.py:148
  38.4 19.9 %collective-permute-done.1.a_pair = bf16[2,7,128,128]{3,2,1,0:T(8,128)(2,1)S(1)} collective-permute-done((bf16[2,7,128,128]{3,2,1,0:T(8,128)(2,1)S(1)}, bf16[2,7,128,128]{3,2,1,0:T(8,128)(2,1)S(1)}, u32[]{:S(2)}, u32[]{:S(2)}) %collective-permute-start.1) | collective-permute-done | bytes 458784 | tf_op jit(solution)/shard_map/ppermute | solution.py:147
  58.3 7.9 %collective-permute-done.2.p_pair = bf16[2,7,128,128]{3,2,1,0:T(8,128)(2,1)S(1)} collective-permute-done((bf16[2,7,128,128]{3,2,1,0:T(8,128)(2,1)S(1)}, bf16[2,7,128,128]{3,2,1,0:T(8,128)(2,1)S(1)}, u32[]{:S(2)}, u32[]{:S(2)}) %collective-permute-start.2) | collective-permute-done | bytes 458784 | tf_op jit(solution)/shard_map/ppermute | solution.py:148
  66.2 0.0 all-to-all-done.gathered_ref
  66.2 0.0 copy-done.2
  66.2 0.0 copy-done.3
  66.2 3.8 %main.1 = s16[16,80,128]{2,1,0:T(8,128)(2,1)S(1)} custom-call(s32[64,7]{1,0:T(8,128)S(1)} %copy-done.2, s32[64]{0:T(128)S(1)} %copy-done.3, s16[16,2,144,128]{3,2,1,0:T(8,128)(2,1)S(1)} %all-to-all-done.gathered_ref, bf16[2,7,128,128]{3,2,1,0:T(8,128)(2,1)S(1)} %copy-done.1, bf16[2,7,128,128]{3,2,1,0:T(8,128)(2,1)S(1)} %copy-done, ...), custom_call_target="tpu_custom_call" | custom-call | tf_op jit(solution)/shard_map/main/pallas_call | solution.py:152
  70.1 14.1 %all_to_all.10.parts_ref = s16[16,80,128]{2,1,0:T(8,128)(2,1)} all-to-all(s16[16,80,128]{2,1,0:T(8,128)(2,1)S(1)} %main.1), channel_id=1, replica_groups=mesh['row'=16,'col'=16,'fiber'=2] {'row'}, dimensions={0} | all-to-all | bytes 655360 | tf_op jit(solution)/shard_map/all_to_all | solution.py:161
  84.2 1.8 %sum.1 = f32[128,128]{1,0:T(8,128)} custom-call(s16[16,80,128]{2,1,0:T(8,128)(2,1)} %all_to_all.10.parts_ref), custom_call_target="tpu_custom_call" | custom-call | tf_op jit(solution)/shard_map/sum/pallas_call | solution.py:162
  85.9 6.3 %collective-permute-start.3 = (f32[128,128]{1,0:T(8,128)}, f32[128,128]{1,0:T(8,128)S(1)}, u32[]{:S(2)}, u32[]{:S(2)}) collective-permute-start(f32[128,128]{1,0:T(8,128)} %sum.1), channel_id=1, source_target_pairs={{0,16},{1,17},{2,18},{3,19},{4,20},{5,21},{6,22},{7,23},{8,24},{9,... | collective-permute-start | bytes 196616 | tf_op jit(solution)/shard_map/ppermute | solution.py:169
  92.2 4.0 %collective-permute-start.4 = (f32[128,128]{1,0:T(8,128)}, f32[128,128]{1,0:T(8,128)S(1)}, u32[]{:S(2)}, u32[]{:S(2)}) collective-permute-start(f32[128,128]{1,0:T(8,128)} %sum.1), channel_id=1, source_target_pairs={{0,17},{1,16},{2,19},{3,18},{4,21},{5,20},{6,23},{7,22},{8,25},{9,... | collective-permute-start | bytes 196616 | tf_op jit(solution)/shard_map/ppermute | solution.py:170
  96.2 0.6 collective-permute-done.3
  96.8 5.7 %collective-permute-done.4 = f32[128,128]{1,0:T(8,128)S(1)} collective-permute-done((f32[128,128]{1,0:T(8,128)}, f32[128,128]{1,0:T(8,128)S(1)}, u32[]{:S(2)}, u32[]{:S(2)}) %collective-permute-start.4) | collective-permute-done | bytes 65568 | tf_op jit(solution)/shard_map/ppermute | solution.py:170
  102.5 0.6 add.3
  (1 shorter events, 0.0 us)
Async XLA Ops:
  3.6 19.3 %collective-permute-start = (s16[2,144,128]{2,1,0:T(8,128)(2,1)}, s16[2,144,128]{2,1,0:T(8,128)(2,1)S(1)}, u32[]{:S(2)}, u32[]{:S(2)}) collective-permute-start(s16[2,144,128]{2,1,0:T(8,128)(2,1)} %get-tuple-element.8), channel_id=1, source_target_pairs={{0,17},{1,16},{2,19},{3,18},{4,21},{5,20},{6,23},{7,22},{8,25},{9,... | collective-permute-start | bytes 221192 | tf_op jit(solution)/shard_map/ppermute | solution.py:146
  25.0 7.5 %copy-start.1 = (bf16[2,7,128,128]{3,2,1,0:T(8,128)(2,1)S(1)}, bf16[2,7,128,128]{3,2,1,0:T(8,128)(2,1)}, u32[]{:S(2)}) copy-start(bf16[2,7,128,128]{3,2,1,0:T(8,128)(2,1)} %a_own.1) | copy-start | bytes 1376260
  25.0 10.9 %copy-start = (bf16[2,7,128,128]{3,2,1,0:T(8,128)(2,1)S(1)}, bf16[2,7,128,128]{3,2,1,0:T(8,128)(2,1)}, u32[]{:S(2)}) copy-start(bf16[2,7,128,128]{3,2,1,0:T(8,128)(2,1)} %p_own.1) | copy-start | bytes 1376260
  25.0 41.2 %copy-start.2 = (s32[64,7]{1,0:T(8,128)S(1)}, s32[64,7]{1,0:T(8,128)}, u32[]{:S(2)}) copy-start(s32[64,7]{1,0:T(8,128)} %copy.7.columns_ref) | copy-start | bytes 5380
  25.0 41.2 %copy-start.3 = (s32[64]{0:T(128)S(1)}, s32[64]{0:T(128)}, u32[]{:S(2)}) copy-start(s32[64]{0:T(128)} %aggregates_ref.3) | copy-start | bytes 772
  25.0 41.2 %all-to-all-start = ((s16[16,2,144,128]{3,2,1,0:T(8,128)(2,1)}), s16[16,2,144,128]{3,2,1,0:T(8,128)(2,1)S(1)}, u32[]{:S(2)}, u32[]{:S(2)}) async-start(s16[16,2,144,128]{3,2,1,0:T(8,128)(2,1)} %bitcast.2), calls=%async_computation | async-start | bytes 2359296 | tf_op jit(solution)/shard_map/all_to_all | solution.py:151
  32.5 25.7 %collective-permute-start.1 = (bf16[2,7,128,128]{3,2,1,0:T(8,128)(2,1)S(1)}, bf16[2,7,128,128]{3,2,1,0:T(8,128)(2,1)S(1)}, u32[]{:S(2)}, u32[]{:S(2)}) collective-permute-start(bf16[2,7,128,128]{3,2,1,0:T(8,128)(2,1)S(1)} %copy-done.1), channel_id=1, source_target_pairs={{0,128},{32,160},{64,192},{96,224},{128,0},{160,32},{192,64},{224,... | collective-permute-start | bytes 1376264 | tf_op jit(solution)/shard_map/ppermute | solution.py:147
  35.9 30.3 %collective-permute-start.2 = (bf16[2,7,128,128]{3,2,1,0:T(8,128)(2,1)S(1)}, bf16[2,7,128,128]{3,2,1,0:T(8,128)(2,1)S(1)}, u32[]{:S(2)}, u32[]{:S(2)}) collective-permute-start(bf16[2,7,128,128]{3,2,1,0:T(8,128)(2,1)S(1)} %copy-done), channel_id=1, source_target_pairs={{0,128},{32,160},{64,192},{96,224},{128,0},{160,32},{192,64},{224,... | collective-permute-start | bytes 1376264 | tf_op jit(solution)/shard_map/ppermute | solution.py:148
  85.9 10.9 %collective-permute-start.3 = (f32[128,128]{1,0:T(8,128)}, f32[128,128]{1,0:T(8,128)S(1)}, u32[]{:S(2)}, u32[]{:S(2)}) collective-permute-start(f32[128,128]{1,0:T(8,128)} %sum.1), channel_id=1, source_target_pairs={{0,16},{1,17},{2,18},{3,19},{4,20},{5,21},{6,22},{7,23},{8,24},{9,... | collective-permute-start | bytes 196616 | tf_op jit(solution)/shard_map/ppermute | solution.py:169
  92.2 10.3 %collective-permute-start.4 = (f32[128,128]{1,0:T(8,128)}, f32[128,128]{1,0:T(8,128)S(1)}, u32[]{:S(2)}, u32[]{:S(2)}) collective-permute-start(f32[128,128]{1,0:T(8,128)} %sum.1), channel_id=1, source_target_pairs={{0,17},{1,16},{2,19},{3,18},{4,21},{5,20},{6,23},{7,22},{8,25},{9,... | collective-permute-start | bytes 196616 | tf_op jit(solution)/shard_map/ppermute | solution.py:170

commit v2 on v1

--- a/solution.py
+++ b/solution.py
@@ -23,7 +23,7 @@
 
 
 def scale_of(codes):
-    exponent = codes.astype(jnp.int32).astype(F32)[0:1]
+    exponent = codes[0:1].astype(F32)
     return jnp.exp2(exponent * (1.0 / STEPS)) * (1.0 / TOP)
 
 
@@ -48,7 +48,7 @@
         first = jnp.zeros((BLK, BLK), F32)
         second = jnp.zeros((BLK, BLK), F32)
         for k in range(slots):
-            group = aggregates_ref[columns_ref[start + q, k]]
+            group = aggregates_ref[columns_ref[k, start + q]]
             term = terms_ref[q, k].astype(F32)
             first = first + term * jnp.where(group == working, 1.0, 0.0)
             second = second + term * jnp.where(group == col, 1.0, 0.0)
@@ -58,11 +58,13 @@
         packed = (jnp.where(low, p0, swap_halves(p1)), jnp.where(low, swap_halves(p0), p1))
         for h in range(2):
             steps, scale = code(packed[h])
-            out_ref[h, 0:BLK, :] = steps
-            out_ref[h, BLK : BLK + SCALE_ROWS, :] = scale
-
-
-def main_kernel(columns_ref, aggregates_ref, gathered_ref, a_own, p_own, a_pair, p_pair, out_ref, total):
+            targets = [r for r in range(own_ref.shape[0]) if r // 4 % 2 == h] if out_ref is own_ref else [h]
+            for target in targets:
+                out_ref[target, 0:BLK, :] = steps
+                out_ref[target, BLK : BLK + SCALE_ROWS, :] = scale
+
+
+def main_kernel(columns_ref, aggregates_ref, near_ref, far_ref, a_own, p_own, a_or_p, p_or_a, out_ref, total):
     rows, slots = a_own.shape[0], a_own.shape[1]
     nfiber = lax.axis_size("fiber")
     fiber = lax.axis_index("fiber")
@@ -70,28 +72,39 @@
     low = low_lanes(BLK)
     lane_half = lax.broadcasted_iota(jnp.int32, (1, BLK), 1) // HALF
     total[...] = jnp.zeros_like(total)
-    for a_ref, p_ref, panel in ((a_own, p_own, row), (a_pair, p_pair, row ^ 4)):
+    first_core = lax.axis_index("col") % 2 == 0
+    for a_ref, p_ref, panel in ((a_own, p_own, row), (a_or_p, p_or_a, row ^ 4)):
+        paired = a_ref is a_or_p
+
+        def blocks(ref, second_core_ref, q, k):
+            if not paired:
+                return ref[q, k]
+            return jnp.where(first_core, ref[q, k], second_core_ref[q, k])
+
         for q in range(rows):
             i = (panel * nfiber + fiber) * rows + q
             y = jnp.zeros((BLK, 2 * BLK), F32)
             for k in range(slots):
-                j = columns_ref[i, k]
+                j = columns_ref[k, i]
                 source = j // 4
                 layer = (j // 2) % 2
-                other = jnp.where(layer == fiber, 0, 1)
-                factor = scale_of(gathered_ref[source, other, BLK : BLK + SCALE_ROWS, :])
-                factor = jnp.where(lane_half == j % 2, factor, 0.0)
-                block = gathered_ref[source, other, 0:BLK, :].astype(jnp.int32).astype(F32) * factor
+                near = layer == fiber
+                block, codes = [
+                    jnp.where(near, near_ref[source, part].astype(jnp.int32), far_ref[source, part].astype(jnp.int32))
+                    for part in (slice(0, BLK), slice(BLK, BLK + SCALE_ROWS))
+                ]
+                factor = jnp.where(lane_half == j % 2, scale_of(codes), 0.0)
+                block = block.astype(F32) * factor
                 high = block.astype(BF16)
                 rest = (block - high.astype(F32)).astype(BF16)
-                y = y + jnp.dot(a_ref[q, k], jnp.concatenate([high, rest], axis=1), preferred_element_type=F32)
+                y = y + jnp.dot(blocks(a_ref, p_ref, q, k), jnp.concatenate([high, rest], axis=1), preferred_element_type=F32)
             y = y[:, :BLK] + y[:, BLK:]
             y = y + swap_halves(y)
             high = y.astype(BF16).astype(F32)
             split = jnp.where(low, high, y - high).astype(BF16)
             for k in range(slots):
-                group = aggregates_ref[columns_ref[i, k]]
-                lifted = lax.dot_general(p_ref[q, k], split, (((0,), (0,)), ((), ())), preferred_element_type=F32)
+                group = aggregates_ref[columns_ref[k, i]]
+                lifted = lax.dot_general(blocks(p_ref, a_ref, q, k), split, (((0,), (0,)), ((), ())), preferred_element_type=F32)
                 total[group] += lifted
     low = low_lanes(HALF)
     for coarse in range(total.shape[0]):
@@ -107,7 +120,7 @@
     halves = [jnp.zeros((HALF, BLK), F32), jnp.zeros((HALF, BLK), F32)]
     for source in range(parts_ref.shape[0]):
         h = (source // 4) % 2
-        factor = scale_of(parts_ref[source, HALF : HALF + SCALE_ROWS, :])
+        factor = scale_of(parts_ref[source, HALF : HALF + SCALE_ROWS, :].astype(jnp.int32))
         halves[h] = halves[h] + parts_ref[source, 0:HALF, :].astype(jnp.int32).astype(F32) * factor
     left, right = halves
     out_ref[0:HALF, :] = jnp.where(low, left, swap_halves(right))
@@ -135,29 +148,34 @@
     across = [
         (c * nfiber + f, (c + ncol // 2) % ncol * nfiber + 1 - f) for c in range(ncol) for f in range(nfiber)
     ]
-    unit = jax.ShapeDtypeStruct((2, BLK + SCALE_ROWS, BLK), jnp.int16)
+    columns = block_columns.T
+    packed_rows = BLK + SCALE_ROWS
+    here = jnp.where(lax.axis_index("col") % 2 == 0, a_blocks, p_terms)
+    from_pair = lax.ppermute(here, "row", pairs)
     own, partner = pl.pallas_call(
         build_kernel,
-        out_shape=(unit, unit),
+        out_shape=(
+            jax.ShapeDtypeStruct((nrow, packed_rows, BLK), jnp.int16),
+            jax.ShapeDtypeStruct((2, packed_rows, BLK), jnp.int16),
+        ),
         in_specs=[SMEM, SMEM, VMEM],
         out_specs=(VMEM, VMEM),
         name="build",
-    )(block_columns, aggregates, p_terms)
+    )(columns, aggregates, p_terms)
     crossed = lax.ppermute(partner, ("col", "fiber"), across)
-    a_pair = lax.ppermute(a_blocks, "row", pairs)
-    p_pair = lax.ppermute(p_terms, "row", pairs)
-    both = jnp.stack([own, crossed], axis=1)
-    sent = jnp.broadcast_to(both[None, :, None], (nrow // 8, 2, 4) + both.shape[1:]).reshape((nrow,) + both.shape[1:])
-    gathered = lax.all_to_all(sent, "row", 0, 0, tiled=True)
+    near = lax.all_to_all(own, "row", 0, 0, tiled=True)
+    crossed = jnp.broadcast_to(crossed[None, :, None], (nrow // 8, 2, 4, packed_rows, BLK))
+    far = lax.all_to_all(crossed.reshape(nrow, packed_rows, BLK), "row", 0, 0, tiled=True)
+    from_core = lax.ppermute(from_pair, "col", [(c, c ^ 1) for c in range(ncol)])
     parts = pl.pallas_call(
         main_kernel,
         out_shape=jax.ShapeDtypeStruct((nrow, HALF + SCALE_ROWS, BLK), jnp.int16),
-        in_specs=[SMEM, SMEM] + [VMEM] * 5,
+        in_specs=[SMEM, SMEM] + [VMEM] * 6,
         out_specs=VMEM,
         scratch_shapes=[pltpu.VMEM((nrow, BLK, BLK), F32)],
         compiler_params=pltpu.CompilerParams(vmem_limit_bytes=32 * 1024 * 1024),
         name="main",
-    )(block_columns, aggregates, gathered, a_blocks, p_terms, a_pair, p_pair)
+    )(columns, aggregates, near, far, a_blocks, p_terms, from_pair, from_core)
     received = lax.all_to_all(parts, "row", 0, 0, tiled=True)
     tile = pl.pallas_call(
         sum_kernel,

time: 104 us -> 85 us (0.82)
  waiting for transfers between devices: 40.7 us -> 20.3 us
  starting transfers between devices: 36.3 us -> 43 us
  blocking collectives: 14.1 us -> 12.1 us
  local copies, waits for them, and re-layouts: 2.59 us -> 0.92 us
    ppermute x2, waiting for transfers between devices: 27.8 us -> 0.01 us  [the longest x1 0.01 us: local(): from_pair = lax.ppermute(here, 'row', pairs)]
    all_to_all x1 -> x2, starting transfers between devices: 7.54 us -> 16.4 us  [the longest x1 9.32 us: local(): near = lax.all_to_all(own, 'row', 0, 0, tiled=True)]
    all_to_all x1 -> x2, waiting for transfers between devices: 0.01 us -> 8.36 us  [the longest x1 8.35 us: local(): lax.all_to_all(crossed.reshape(nrow, packed_rows, BLK), 'row', 0, 0, tile...]
    all_to_all x1, blocking collectives: 14.1 us -> 12.1 us  [local(): received = lax.all_to_all(parts, 'row', 0, 0, tiled=True)]
    ppermute x1, starting transfers between devices: 12.7 us -> 10.9 us  [local(): crossed = lax.ppermute(partner, ('col', 'fiber'), across)]
    unnamed x9 -> x10, local copies, waits for them, and re-layouts: 1.4 us -> 0.02 us
    ppermute x1, waiting for transfers between devices: 6.59 us -> 5.44 us  [local(): crossed = lax.ppermute(partner, ('col', 'fiber'), across)]
  transfers between devices with their start and end apart: 6 -> 7, of which waited for: 5 -> 4; matrix products, arithmetic and copies ran while one was open for 0% -> 1% of each run, Pallas kernels for 0% -> 0%
where the time goes in v2:
time: 85 us; the launch traced here: 84.4 us
  starting transfers between devices  43 us (51%)
  waiting for transfers between devices  20.3 us (24%)
  blocking collectives  12.1 us (14%)
  Pallas kernels  7.36 us (9%)
  local copies, waits for them, and re-layouts  0.92 us (1%)
    all_to_all x1, blocking collectives, local(): received = lax.all_to_all(parts, 'row', 0, 0, tiled=True)  12.1 us
    ppermute x1, starting transfers between devices, local(): crossed = lax.ppermute(partner, ('col', 'fiber'), across)  10.9 us
    all_to_all x1, starting transfers between devices, local(): near = lax.all_to_all(own, 'row', 0, 0, tiled=True)  9.32 us
    all_to_all x1, waiting for transfers between devices, local(): lax.all_to_all(crossed.reshape(nrow, packed_rows, BLK), 'row', 0, 0, tile...  8.35 us
    all_to_all x1, starting transfers between devices, local(): lax.all_to_all(crossed.reshape(nrow, packed_rows, BLK), 'row', 0, 0, tile...  7.06 us
    ppermute x1, starting transfers between devices, local(): up = lax.ppermute(tile, ('col', 'fiber'), along(ncol // 4))  6.36 us
    ppermute x1, waiting for transfers between devices, local(): crossed = lax.ppermute(partner, ('col', 'fiber'), across)  5.44 us
    ppermute x1, waiting for transfers between devices, local(): down = lax.ppermute(tile, ('col', 'fiber'), along(-(ncol // 4)))  5.03 us
  transfers between devices with their start and end apart: 7, of which 4 were waited for; matrix products, arithmetic and copies ran while one was open for 1% of the time, Pallas kernels for 0%

profile of v2, /device:TPU:8, one launch (start us, length us, event | category | flops | bytes accessed | tf_op | source)
XLA Modules:
  0.0 84.4 jit_solution(9128773190020827844)
XLA Ops:
  0.0 2.2 %build.1 = (s16[16,144,128]{2,1,0:T(8,128)(2,1)}, s16[2,144,128]{2,1,0:T(8,128)(2,1)}) custom-call(s32[7,64]{1,0:T(8,128)} %bitcast.2, s32[64]{0:T(128)} %aggregates_ref.3, bf16[2,7,128,128]{3,2,1,0:T(8,128)(2,1)} %p_own.1), custom_call_target="tpu_custom_call" | custom-call | tf_op jit(solution)/shard_map/build/pallas_call | solution.py:155
  2.2 0.0 copy-start
  2.2 0.0 copy-start.1
  2.2 9.3 %all-to-all-start = ((s16[16,144,128]{2,1,0:T(8,128)(2,1)}), s16[16,144,128]{2,1,0:T(8,128)(2,1)S(1)}, u32[]{:S(2)}, u32[]{:S(2)}) async-start(s16[16,144,128]{2,1,0:T(8,128)(2,1)} %get-tuple-element.7), calls=%async_computation | async-start | bytes 1179648 | tf_op jit(solution)/shard_map/all_to_all | solution.py:166
  11.6 0.0 copy-done
  11.6 0.0 copy-done.1
  11.6 0.0 copy-start.4
  11.6 0.1 broadcast_select_fusion
  11.6 3.4 %collective-permute-start.1 = (bf16[2,7,128,128]{3,2,1,0:T(8,128)(2,1)S(1)}, bf16[2,7,128,128]{3,2,1,0:T(8,128)(2,1)S(1)}, u32[]{:S(2)}, u32[]{:S(2)}) collective-permute-start(bf16[2,7,128,128]{3,2,1,0:T(8,128)(2,1)S(1)} %broadcast_select_fusion), channel_id=1, source_target_pairs={{0,128},{32,160},{64,192},{96,224},{128,0},{160,32},{192,64},{224,... | collective-permute-start | bytes 1376264 | tf_op jit(solution)/shard_map/ppermute | solution.py:154
  15.1 0.0 copy-done.4
  15.1 10.9 %collective-permute-start = (s16[2,144,128]{2,1,0:T(8,128)(2,1)S(1)}, s16[2,144,128]{2,1,0:T(8,128)(2,1)S(1)}, u32[]{:S(2)}, u32[]{:S(2)}) collective-permute-start(s16[2,144,128]{2,1,0:T(8,128)(2,1)S(1)} %copy-done.4), channel_id=1, source_target_pairs={{0,17},{1,16},{2,19},{3,18},{4,21},{5,20},{6,23},{7,22},{8,25},{9,... | collective-permute-start | bytes 221192 | tf_op jit(solution)/shard_map/ppermute | solution.py:165
  26.0 5.4 %collective-permute-done = s16[2,144,128]{2,1,0:T(8,128)(2,1)S(1)} collective-permute-done((s16[2,144,128]{2,1,0:T(8,128)(2,1)S(1)}, s16[2,144,128]{2,1,0:T(8,128)(2,1)S(1)}, u32[]{:S(2)}, u32[]{:S(2)}) %collective-permute-start) | collective-permute-done | bytes 73760 | tf_op jit(solution)/shard_map/ppermute | solution.py:165
  31.4 0.0 all-to-all-done.near_ref
  31.4 0.9 %broadcast_in_dim.2 = s16[2,2,4,144,128]{4,3,2,1,0:T(8,128)(2,1)} broadcast(s16[2,144,128]{2,1,0:T(8,128)(2,1)S(1)} %collective-permute-done), dimensions={1,3,4} | broadcast | bytes 663552 | tf_op jit(solution)/shard_map/broadcast_in_dim | solution.py:167
  32.3 0.0 copy-start.2
  32.3 0.0 copy-start.3
  32.3 7.1 %all-to-all-start.1 = ((s16[16,144,128]{2,1,0:T(8,128)(2,1)}), s16[16,144,128]{2,1,0:T(8,128)(2,1)S(1)}, u32[]{:S(2)}, u32[]{:S(2)}) async-start(s16[16,144,128]{2,1,0:T(8,128)(2,1)} %bitcast.1), calls=%async_computation.1 | async-start | bytes 1179648 | tf_op jit(solution)/shard_map/all_to_all | solution.py:168
  39.4 0.0 collective-permute-done.1.a_or_p
  39.4 1.9 %collective-permute-start.2 = (bf16[2,7,128,128]{3,2,1,0:T(8,128)(2,1)S(1)}, bf16[2,7,128,128]{3,2,1,0:T(8,128)(2,1)S(1)}, u32[]{:S(2)}, u32[]{:S(2)}) collective-permute-start(bf16[2,7,128,128]{3,2,1,0:T(8,128)(2,1)S(1)} %collective-permute-done.1.a_or_p), channel_id=1, source_target_pairs={{0,2},{2,0},{4,6},{6,4},{8,10},{10,8},{12,14},{14,12},{16,18},{18,... | collective-permute-start | bytes 1376264 | tf_op jit(solution)/shard_map/ppermute | solution.py:169
  41.3 8.4 %all-to-all-done.1.far_ref = s16[16,144,128]{2,1,0:T(8,128)(2,1)S(1)} async-done(((s16[16,144,128]{2,1,0:T(8,128)(2,1)}), s16[16,144,128]{2,1,0:T(8,128)(2,1)S(1)}, u32[]{:S(2)}, u32[]{:S(2)}) %all-to-all-start.1) | async-done | bytes 589856 | tf_op jit(solution)/shard_map/all_to_all | solution.py:168
  49.7 0.0 collective-permute-done.2.p_or_a
  49.7 0.0 copy-done.2
  49.7 0.0 copy-done.3
  49.7 3.4 %main.1 = s16[16,80,128]{2,1,0:T(8,128)(2,1)S(1)} custom-call(s32[7,64]{1,0:T(8,128)S(1)} %bitcast.3, s32[64]{0:T(128)S(1)} %copy-done.3, s16[16,144,128]{2,1,0:T(8,128)(2,1)S(1)} %all-to-all-done.near_ref, s16[16,144,128]{2,1,0:T(8,128)(2,1)S(1)} %all-to-all-done.1.far_ref, bf16[2,7,128,128]{3,2,1,0:T(8,128)(2,1)S(1)} %copy-done.1, ...), custom_call_target="tpu_custom_call" | custom-call | tf_op jit(solution)/shard_map/main/pallas_call | solution.py:170
  53.1 12.1 %all_to_all.15.parts_ref = s16[16,80,128]{2,1,0:T(8,128)(2,1)} all-to-all(s16[16,80,128]{2,1,0:T(8,128)(2,1)S(1)} %main.1), channel_id=1, replica_groups=mesh['row'=16,'col'=16,'fiber'=2] {'row'}, dimensions={0} | all-to-all | bytes 655360 | tf_op jit(solution)/shard_map/all_to_all | solution.py:179
  65.1 1.8 %sum.1 = f32[128,128]{1,0:T(8,128)} custom-call(s16[16,80,128]{2,1,0:T(8,128)(2,1)} %all_to_all.15.parts_ref), custom_call_target="tpu_custom_call" | custom-call | tf_op jit(solution)/shard_map/sum/pallas_call | solution.py:180
  66.9 6.4 %collective-permute-start.3 = (f32[128,128]{1,0:T(8,128)}, f32[128,128]{1,0:T(8,128)S(1)}, u32[]{:S(2)}, u32[]{:S(2)}) collective-permute-start(f32[128,128]{1,0:T(8,128)} %sum.1), channel_id=1, source_target_pairs={{0,16},{1,17},{2,18},{3,19},{4,20},{5,21},{6,22},{7,23},{8,24},{9,... | collective-permute-start | bytes 196616 | tf_op jit(solution)/shard_map/ppermute | solution.py:187
  73.3 4.0 %collective-permute-start.4 = (f32[128,128]{1,0:T(8,128)}, f32[128,128]{1,0:T(8,128)S(1)}, u32[]{:S(2)}, u32[]{:S(2)}) collective-permute-start(f32[128,128]{1,0:T(8,128)} %sum.1), channel_id=1, source_target_pairs={{0,17},{1,16},{2,19},{3,18},{4,21},{5,20},{6,23},{7,22},{8,25},{9,... | collective-permute-start | bytes 196616 | tf_op jit(solution)/shard_map/ppermute | solution.py:188
  77.3 1.5 %collective-permute-done.3 = f32[128,128]{1,0:T(8,128)S(1)} collective-permute-done((f32[128,128]{1,0:T(8,128)}, f32[128,128]{1,0:T(8,128)S(1)}, u32[]{:S(2)}, u32[]{:S(2)}) %collective-permute-start.3) | collective-permute-done | bytes 65568 | tf_op jit(solution)/shard_map/ppermute | solution.py:187
  78.7 5.0 %collective-permute-done.4 = f32[128,128]{1,0:T(8,128)S(1)} collective-permute-done((f32[128,128]{1,0:T(8,128)}, f32[128,128]{1,0:T(8,128)S(1)}, u32[]{:S(2)}, u32[]{:S(2)}) %collective-permute-start.4) | collective-permute-done | bytes 65568 | tf_op jit(solution)/shard_map/ppermute | solution.py:188
  83.8 0.6 add.8
Async XLA Ops:
  2.2 9.3 %copy-start = (bf16[2,7,128,128]{3,2,1,0:T(8,128)(2,1)S(1)}, bf16[2,7,128,128]{3,2,1,0:T(8,128)(2,1)}, u32[]{:S(2)}) copy-start(bf16[2,7,128,128]{3,2,1,0:T(8,128)(2,1)} %p_own.1) | copy-start | bytes 1376260
  2.2 9.3 %copy-start.1 = (bf16[2,7,128,128]{3,2,1,0:T(8,128)(2,1)S(1)}, bf16[2,7,128,128]{3,2,1,0:T(8,128)(2,1)}, u32[]{:S(2)}) copy-start(bf16[2,7,128,128]{3,2,1,0:T(8,128)(2,1)} %a_own.1) | copy-start | bytes 1376260
  2.2 29.2 %all-to-all-start = ((s16[16,144,128]{2,1,0:T(8,128)(2,1)}), s16[16,144,128]{2,1,0:T(8,128)(2,1)S(1)}, u32[]{:S(2)}, u32[]{:S(2)}) async-start(s16[16,144,128]{2,1,0:T(8,128)(2,1)} %get-tuple-element.7), calls=%async_computation | async-start | bytes 1179648 | tf_op jit(solution)/shard_map/all_to_all | solution.py:166
  11.6 3.5 %copy-start.4 = (s16[2,144,128]{2,1,0:T(8,128)(2,1)S(1)}, s16[2,144,128]{2,1,0:T(8,128)(2,1)}, u32[]{:S(2)}) copy-start(s16[2,144,128]{2,1,0:T(8,128)(2,1)} %get-tuple-element.8) | copy-start | bytes 221188
  11.6 27.7 %collective-permute-start.1 = (bf16[2,7,128,128]{3,2,1,0:T(8,128)(2,1)S(1)}, bf16[2,7,128,128]{3,2,1,0:T(8,128)(2,1)S(1)}, u32[]{:S(2)}, u32[]{:S(2)}) collective-permute-start(bf16[2,7,128,128]{3,2,1,0:T(8,128)(2,1)S(1)} %broadcast_select_fusion), channel_id=1, source_target_pairs={{0,128},{32,160},{64,192},{96,224},{128,0},{160,32},{192,64},{224,... | collective-permute-start | bytes 1376264 | tf_op jit(solution)/shard_map/ppermute | solution.py:154
  15.1 16.4 %collective-permute-start = (s16[2,144,128]{2,1,0:T(8,128)(2,1)S(1)}, s16[2,144,128]{2,1,0:T(8,128)(2,1)S(1)}, u32[]{:S(2)}, u32[]{:S(2)}) collective-permute-start(s16[2,144,128]{2,1,0:T(8,128)(2,1)S(1)} %copy-done.4), channel_id=1, source_target_pairs={{0,17},{1,16},{2,19},{3,18},{4,21},{5,20},{6,23},{7,22},{8,25},{9,... | collective-permute-start | bytes 221192 | tf_op jit(solution)/shard_map/ppermute | solution.py:165
  32.3 17.4 %copy-start.2 = (s32[64,7]{0,1:T(8,128)S(1)}, s32[64,7]{0,1:T(8,128)}, u32[]{:S(2)}) copy-start(s32[64,7]{0,1:T(8,128)} %param.6) | copy-start | bytes 5380
  32.3 17.4 %copy-start.3 = (s32[64]{0:T(128)S(1)}, s32[64]{0:T(128)}, u32[]{:S(2)}) copy-start(s32[64]{0:T(128)} %aggregates_ref.3) | copy-start | bytes 772
  32.3 17.4 %all-to-all-start.1 = ((s16[16,144,128]{2,1,0:T(8,128)(2,1)}), s16[16,144,128]{2,1,0:T(8,128)(2,1)S(1)}, u32[]{:S(2)}, u32[]{:S(2)}) async-start(s16[16,144,128]{2,1,0:T(8,128)(2,1)} %bitcast.1), calls=%async_computation.1 | async-start | bytes 1179648 | tf_op jit(solution)/shard_map/all_to_all | solution.py:168
  39.4 10.3 %collective-permute-start.2 = (bf16[2,7,128,128]{3,2,1,0:T(8,128)(2,1)S(1)}, bf16[2,7,128,128]{3,2,1,0:T(8,128)(2,1)S(1)}, u32[]{:S(2)}, u32[]{:S(2)}) collective-permute-start(bf16[2,7,128,128]{3,2,1,0:T(8,128)(2,1)S(1)} %collective-permute-done.1.a_or_p), channel_id=1, source_target_pairs={{0,2},{2,0},{4,6},{6,4},{8,10},{10,8},{12,14},{14,12},{16,18},{18,... | collective-permute-start | bytes 1376264 | tf_op jit(solution)/shard_map/ppermute | solution.py:169
  66.9 11.8 %collective-permute-start.3 = (f32[128,128]{1,0:T(8,128)}, f32[128,128]{1,0:T(8,128)S(1)}, u32[]{:S(2)}, u32[]{:S(2)}) collective-permute-start(f32[128,128]{1,0:T(8,128)} %sum.1), channel_id=1, source_target_pairs={{0,16},{1,17},{2,18},{3,19},{4,20},{5,21},{6,22},{7,23},{8,24},{9,... | collective-permute-start | bytes 196616 | tf_op jit(solution)/shard_map/ppermute | solution.py:187
  73.3 10.5 %collective-permute-start.4 = (f32[128,128]{1,0:T(8,128)}, f32[128,128]{1,0:T(8,128)S(1)}, u32[]{:S(2)}, u32[]{:S(2)}) collective-permute-start(f32[128,128]{1,0:T(8,128)} %sum.1), channel_id=1, source_target_pairs={{0,17},{1,16},{2,19},{3,18},{4,21},{5,20},{6,23},{7,22},{8,25},{9,... | collective-permute-start | bytes 196616 | tf_op jit(solution)/shard_map/ppermute | solution.py:188

commit v3 on v2

--- a/solution.py
+++ b/solution.py
@@ -35,33 +35,35 @@
     return pltpu.roll(value, HALF, 1)
 
 
-def build_kernel(columns_ref, aggregates_ref, terms_ref, own_ref, partner_ref):
+def build_kernel(columns_ref, aggregates_ref, terms_ref, partner_ref, own_ref):
     rows, slots = terms_ref.shape[0], terms_ref.shape[1]
-    nfiber = lax.axis_size("fiber")
     ncol = lax.axis_size("col")
     col = lax.axis_index("col")
-    start = (lax.axis_index("row") * nfiber + lax.axis_index("fiber")) * rows
-    working = lax.rem(col + ncol // 2, ncol)
+    start = (lax.axis_index("row") * lax.axis_size("fiber") + lax.axis_index("fiber")) * rows
     low = low_lanes(BLK)
+    wanted = (col, lax.rem(col + ncol // 2, ncol))
     sums = [[], []]
     for q in range(rows):
-        first = jnp.zeros((BLK, BLK), F32)
-        second = jnp.zeros((BLK, BLK), F32)
+        totals = [jnp.zeros((BLK, BLK), F32) for column in wanted]
         for k in range(slots):
             group = aggregates_ref[columns_ref[k, start + q]]
             term = terms_ref[q, k].astype(F32)
-            first = first + term * jnp.where(group == working, 1.0, 0.0)
-            second = second + term * jnp.where(group == col, 1.0, 0.0)
-        sums[0].append(first)
-        sums[1].append(second)
-    for out_ref, (p0, p1) in zip((own_ref, partner_ref), sums):
+            totals = [t + term * jnp.where(group == column, 1.0, 0.0) for t, column in zip(totals, wanted)]
+        for side, total in zip(sums, totals):
+            side.append(total)
+    for out_ref, (p0, p1) in zip((partner_ref, own_ref), sums):
         packed = (jnp.where(low, p0, swap_halves(p1)), jnp.where(low, swap_halves(p0), p1))
         for h in range(2):
             steps, scale = code(packed[h])
-            targets = [r for r in range(own_ref.shape[0]) if r // 4 % 2 == h] if out_ref is own_ref else [h]
-            for target in targets:
-                out_ref[target, 0:BLK, :] = steps
-                out_ref[target, BLK : BLK + SCALE_ROWS, :] = scale
+            for target in range(out_ref.shape[0]):
+                if out_ref is partner_ref and target == h or out_ref is own_ref and target // 4 % 2 == h:
+                    out_ref[target, 0:BLK, :] = steps
+                    out_ref[target, BLK : BLK + SCALE_ROWS, :] = scale
+
+
+def spread_kernel(pair_ref, out_ref):
+    for target in range(out_ref.shape[0]):
+        out_ref[target] = pair_ref[target // 4 % 2]
 
 
 def main_kernel(columns_ref, aggregates_ref, near_ref, far_ref, a_own, p_own, a_or_p, p_or_a, out_ref, total):
@@ -150,22 +152,30 @@
     ]
     columns = block_columns.T
     packed_rows = BLK + SCALE_ROWS
-    here = jnp.where(lax.axis_index("col") % 2 == 0, a_blocks, p_terms)
-    from_pair = lax.ppermute(here, "row", pairs)
-    own, partner = pl.pallas_call(
+    partner, own = pl.pallas_call(
         build_kernel,
         out_shape=(
+            jax.ShapeDtypeStruct((2, packed_rows, BLK), jnp.int16),
             jax.ShapeDtypeStruct((nrow, packed_rows, BLK), jnp.int16),
-            jax.ShapeDtypeStruct((2, packed_rows, BLK), jnp.int16),
         ),
         in_specs=[SMEM, SMEM, VMEM],
         out_specs=(VMEM, VMEM),
         name="build",
     )(columns, aggregates, p_terms)
+    here = jnp.where(lax.axis_index("col") % 2 == 0, a_blocks, p_terms)
+    from_pair = lax.ppermute(here, "row", pairs)
     crossed = lax.ppermute(partner, ("col", "fiber"), across)
     near = lax.all_to_all(own, "row", 0, 0, tiled=True)
-    crossed = jnp.broadcast_to(crossed[None, :, None], (nrow // 8, 2, 4, packed_rows, BLK))
-    far = lax.all_to_all(crossed.reshape(nrow, packed_rows, BLK), "row", 0, 0, tiled=True)
+    spread = pl.pallas_call(
+        spread_kernel,
+        out_shape=jax.ShapeDtypeStruct((nrow, packed_rows, BLK), jnp.int16),
+        in_specs=[VMEM],
+        out_specs=VMEM,
+        cost_estimate=pl.CostEstimate(flops=2**37, bytes_accessed=2**21, transcendentals=0),
+        compiler_params=pltpu.CompilerParams(vmem_limit_bytes=4 * 1024 * 1024),
+        name="spread",
+    )(crossed)
+    far = lax.all_to_all(spread, "row", 0, 0, tiled=True)
     from_core = lax.ppermute(from_pair, "col", [(c, c ^ 1) for c in range(ncol)])
     parts = pl.pallas_call(
         main_kernel,
@@ -173,7 +183,7 @@
         in_specs=[SMEM, SMEM] + [VMEM] * 6,
         out_specs=VMEM,
         scratch_shapes=[pltpu.VMEM((nrow, BLK, BLK), F32)],
-        compiler_params=pltpu.CompilerParams(vmem_limit_bytes=32 * 1024 * 1024),
+        compiler_params=pltpu.CompilerParams(vmem_limit_bytes=16 * 1024 * 1024),
         name="main",
     )(columns, aggregates, near, far, a_blocks, p_terms, from_pair, from_core)
     received = lax.all_to_all(parts, "row", 0, 0, tiled=True)
@@ -182,6 +192,7 @@
         out_shape=jax.ShapeDtypeStruct((BLK, BLK), F32),
         in_specs=[VMEM],
         out_specs=VMEM,
+        compiler_params=pltpu.CompilerParams(vmem_limit_bytes=4 * 1024 * 1024),
         name="sum",
     )(received)
     up = lax.ppermute(tile, ("col", "fiber"), along(ncol // 4))

time: 85 us -> 80.1 us (0.942)
  waiting for transfers between devices: 20.3 us -> 16.9 us
  local copies, waits for them, and re-layouts: 0.92 us -> 0.02 us
    ppermute x1, waiting for transfers between devices: 5.44 us -> 2.25 us  [local(): crossed = lax.ppermute(partner, ('col', 'fiber'), across)]
    pallas_call x1, Pallas kernels: 1.75 us -> 0.15 us  [local(): pl.pallas_call(sum_kernel, out_shape=jax.ShapeDtypeStruct((BLK, BLK), F32...]
    pallas_call x1 -> x2, Pallas kernels: 2.23 us -> 3.14 us  [the longest x1 2.24 us: local(): pl.pallas_call(build_kernel, out_shape=(jax.ShapeDtypeStruct((2, packed_r...]
    broadcast_in_dim x1 -> x0, local copies, waits for them, and re-layouts: 0.9 us -> none  [local(): jnp.broadcast_to(crossed[None, :, None], (nrow // 8, 2, 4, packed_rows, B...]
  transfers between devices with their start and end apart: 7 -> 7, of which waited for: 4 -> 4; matrix products, arithmetic and copies ran while one was open for 1% -> 0% of each run, Pallas kernels for 0% -> 1%
where the time goes in v3:
time: 80.1 us; the launch traced here: 79.6 us
  starting transfers between devices  43.3 us (54%)
  waiting for transfers between devices  16.9 us (21%)
  blocking collectives  11.9 us (15%)
  Pallas kernels  6.68 us (8%)
    all_to_all x1, blocking collectives, local(): received = lax.all_to_all(parts, 'row', 0, 0, tiled=True)  11.9 us
    ppermute x1, starting transfers between devices, local(): crossed = lax.ppermute(partner, ('col', 'fiber'), across)  10.9 us
    all_to_all x1, starting transfers between devices, local(): near = lax.all_to_all(own, 'row', 0, 0, tiled=True)  9.34 us
    all_to_all x1, waiting for transfers between devices, local(): far = lax.all_to_all(spread, 'row', 0, 0, tiled=True)  8.35 us
    all_to_all x1, starting transfers between devices, local(): far = lax.all_to_all(spread, 'row', 0, 0, tiled=True)  7.36 us
    ppermute x1, starting transfers between devices, local(): up = lax.ppermute(tile, ('col', 'fiber'), along(ncol // 4))  6.38 us
    ppermute x1, waiting for transfers between devices, local(): down = lax.ppermute(tile, ('col', 'fiber'), along(-(ncol // 4)))  5.04 us
    ppermute x1, starting transfers between devices, local(): down = lax.ppermute(tile, ('col', 'fiber'), along(-(ncol // 4)))  4 us
  transfers between devices with their start and end apart: 7, of which 4 were waited for; matrix products, arithmetic and copies ran while one was open for 0% of the time, Pallas kernels for 1%

profile of v3, /device:TPU:8, one launch (start us, length us, event | category | flops | bytes accessed | tf_op | source)
XLA Modules:
  0.0 79.6 jit_solution(10791547851825994908)
XLA Ops:
  0.0 2.2 %build.1 = (s16[2,144,128]{2,1,0:T(8,128)(2,1)}, s16[16,144,128]{2,1,0:T(8,128)(2,1)}) custom-call(s32[7,64]{1,0:T(8,128)} %bitcast.1, s32[64]{0:T(128)} %aggregates_ref.3, bf16[2,7,128,128]{3,2,1,0:T(8,128)(2,1)} %p_own.1), custom_call_target="tpu_custom_call" | custom-call | tf_op jit(solution)/shard_map/build/pallas_call | solution.py:155
  2.2 0.0 copy-start.4
  2.2 0.0 copy-start
  2.2 0.0 copy-start.1
  2.2 9.3 %all-to-all-start = ((s16[16,144,128]{2,1,0:T(8,128)(2,1)}), s16[16,144,128]{2,1,0:T(8,128)(2,1)S(1)}, u32[]{:S(2)}, u32[]{:S(2)}) async-start(s16[16,144,128]{2,1,0:T(8,128)(2,1)} %get-tuple-element.7), calls=%async_computation | async-start | bytes 1179648 | tf_op jit(solution)/shard_map/all_to_all | solution.py:168
  11.6 0.0 copy-done.4
  11.6 10.9 %collective-permute-start = (s16[2,144,128]{2,1,0:T(8,128)(2,1)S(1)}, s16[2,144,128]{2,1,0:T(8,128)(2,1)S(1)}, u32[]{:S(2)}, u32[]{:S(2)}) collective-permute-start(s16[2,144,128]{2,1,0:T(8,128)(2,1)S(1)} %copy-done.4), channel_id=1, source_target_pairs={{0,17},{1,16},{2,19},{3,18},{4,21},{5,20},{6,23},{7,22},{8,25},{9,... | collective-permute-start | bytes 221192 | tf_op jit(solution)/shard_map/ppermute | solution.py:167
  22.5 0.0 copy-done
  22.6 0.0 copy-done.1
  22.6 0.1 broadcast_select_fusion
  22.6 3.4 %collective-permute-start.1 = (bf16[2,7,128,128]{3,2,1,0:T(8,128)(2,1)S(1)}, bf16[2,7,128,128]{3,2,1,0:T(8,128)(2,1)S(1)}, u32[]{:S(2)}, u32[]{:S(2)}) collective-permute-start(bf16[2,7,128,128]{3,2,1,0:T(8,128)(2,1)S(1)} %broadcast_select_fusion), channel_id=1, source_target_pairs={{0,128},{32,160},{64,192},{96,224},{128,0},{160,32},{192,64},{224,... | collective-permute-start | bytes 1376264 | tf_op jit(solution)/shard_map/ppermute | solution.py:166
  26.0 2.2 %collective-permute-done.pair_ref = s16[2,144,128]{2,1,0:T(8,128)(2,1)S(1)} collective-permute-done((s16[2,144,128]{2,1,0:T(8,128)(2,1)S(1)}, s16[2,144,128]{2,1,0:T(8,128)(2,1)S(1)}, u32[]{:S(2)}, u32[]{:S(2)}) %collective-permute-start) | collective-permute-done | bytes 73760 | tf_op jit(solution)/shard_map/ppermute | solution.py:167
  28.2 0.9 %spread.1 = s16[16,144,128]{2,1,0:T(8,128)(2,1)} custom-call(s16[2,144,128]{2,1,0:T(8,128)(2,1)S(1)} %collective-permute-done.pair_ref), custom_call_target="tpu_custom_call" | custom-call | flops 137438953472 | bytes 2097152 | tf_op jit(solution)/shard_map/spread/pallas_call | solution.py:169
  29.2 0.0 copy-start.2
  29.2 0.0 copy-start.3
  29.2 0.0 all-to-all-done.near_ref
  29.2 7.4 %all-to-all-start.1 = ((s16[16,144,128]{2,1,0:T(8,128)(2,1)}), s16[16,144,128]{2,1,0:T(8,128)(2,1)S(1)}, u32[]{:S(2)}, u32[]{:S(2)}) async-start(s16[16,144,128]{2,1,0:T(8,128)(2,1)} %spread.1), calls=%async_computation.1 | async-start | bytes 1179648 | tf_op jit(solution)/shard_map/all_to_all | solution.py:178
  36.5 0.0 collective-permute-done.1.a_or_p
  36.5 1.9 %collective-permute-start.2 = (bf16[2,7,128,128]{3,2,1,0:T(8,128)(2,1)S(1)}, bf16[2,7,128,128]{3,2,1,0:T(8,128)(2,1)S(1)}, u32[]{:S(2)}, u32[]{:S(2)}) collective-permute-start(bf16[2,7,128,128]{3,2,1,0:T(8,128)(2,1)S(1)} %collective-permute-done.1.a_or_p), channel_id=1, source_target_pairs={{0,2},{2,0},{4,6},{6,4},{8,10},{10,8},{12,14},{14,12},{16,18},{18,... | collective-permute-start | bytes 1376264 | tf_op jit(solution)/shard_map/ppermute | solution.py:179
  38.5 8.4 %all-to-all-done.1.far_ref = s16[16,144,128]{2,1,0:T(8,128)(2,1)S(1)} async-done(((s16[16,144,128]{2,1,0:T(8,128)(2,1)}), s16[16,144,128]{2,1,0:T(8,128)(2,1)S(1)}, u32[]{:S(2)}, u32[]{:S(2)}) %all-to-all-start.1) | async-done | bytes 589856 | tf_op jit(solution)/shard_map/all_to_all | solution.py:178
  46.8 0.0 collective-permute-done.2.p_or_a
  46.8 0.0 copy-done.2
  46.8 0.0 copy-done.3
  46.8 3.4 %main.1 = s16[16,80,128]{2,1,0:T(8,128)(2,1)S(1)} custom-call(s32[7,64]{1,0:T(8,128)S(1)} %bitcast.2, s32[64]{0:T(128)S(1)} %copy-done.3, s16[16,144,128]{2,1,0:T(8,128)(2,1)S(1)} %all-to-all-done.near_ref, s16[16,144,128]{2,1,0:T(8,128)(2,1)S(1)} %all-to-all-done.1.far_ref, bf16[2,7,128,128]{3,2,1,0:T(8,128)(2,1)S(1)} %copy-done.1, ...), custom_call_target="tpu_custom_call" | custom-call | tf_op jit(solution)/shard_map/main/pallas_call | solution.py:180
  50.2 11.9 %all_to_all.15.parts_ref = s16[16,80,128]{2,1,0:T(8,128)(2,1)S(1)} all-to-all(s16[16,80,128]{2,1,0:T(8,128)(2,1)S(1)} %main.1), channel_id=1, replica_groups=mesh['row'=16,'col'=16,'fiber'=2] {'row'}, dimensions={0} | all-to-all | bytes 655360 | tf_op jit(solution)/shard_map/all_to_all | solution.py:189
  62.2 0.2 sum.1
  62.3 6.4 %collective-permute-start.3 = (f32[128,128]{1,0:T(8,128)S(1)}, f32[128,128]{1,0:T(8,128)S(1)}, u32[]{:S(2)}, u32[]{:S(2)}) collective-permute-start(f32[128,128]{1,0:T(8,128)S(1)} %sum.1), channel_id=1, source_target_pairs={{0,16},{1,17},{2,18},{3,19},{4,20},{5,21},{6,22},{7,23},{8,24},{9,... | collective-permute-start | bytes 196616 | tf_op jit(solution)/shard_map/ppermute | solution.py:198
  68.7 4.0 %collective-permute-start.4 = (f32[128,128]{1,0:T(8,128)S(1)}, f32[128,128]{1,0:T(8,128)S(1)}, u32[]{:S(2)}, u32[]{:S(2)}) collective-permute-start(f32[128,128]{1,0:T(8,128)S(1)} %sum.1), channel_id=1, source_target_pairs={{0,17},{1,16},{2,19},{3,18},{4,21},{5,20},{6,23},{7,22},{8,25},{9,... | collective-permute-start | bytes 196616 | tf_op jit(solution)/shard_map/ppermute | solution.py:199
  72.7 1.2 %collective-permute-done.3 = f32[128,128]{1,0:T(8,128)S(1)} collective-permute-done((f32[128,128]{1,0:T(8,128)S(1)}, f32[128,128]{1,0:T(8,128)S(1)}, u32[]{:S(2)}, u32[]{:S(2)}) %collective-permute-start.3) | collective-permute-done | bytes 65568 | tf_op jit(solution)/shard_map/ppermute | solution.py:198
  73.9 5.0 %collective-permute-done.4 = f32[128,128]{1,0:T(8,128)S(1)} collective-permute-done((f32[128,128]{1,0:T(8,128)S(1)}, f32[128,128]{1,0:T(8,128)S(1)}, u32[]{:S(2)}, u32[]{:S(2)}) %collective-permute-start.4) | collective-permute-done | bytes 65568 | tf_op jit(solution)/shard_map/ppermute | solution.py:199
  79.0 0.6 add.8
Async XLA Ops:
  2.2 9.3 %copy-start.4 = (s16[2,144,128]{2,1,0:T(8,128)(2,1)S(1)}, s16[2,144,128]{2,1,0:T(8,128)(2,1)}, u32[]{:S(2)}) copy-start(s16[2,144,128]{2,1,0:T(8,128)(2,1)} %get-tuple-element.8) | copy-start | bytes 221188
  2.2 20.3 %copy-start = (bf16[2,7,128,128]{3,2,1,0:T(8,128)(2,1)S(1)}, bf16[2,7,128,128]{3,2,1,0:T(8,128)(2,1)}, u32[]{:S(2)}) copy-start(bf16[2,7,128,128]{3,2,1,0:T(8,128)(2,1)} %p_own.1) | copy-start | bytes 1376260
  2.2 20.3 %copy-start.1 = (bf16[2,7,128,128]{3,2,1,0:T(8,128)(2,1)S(1)}, bf16[2,7,128,128]{3,2,1,0:T(8,128)(2,1)}, u32[]{:S(2)}) copy-start(bf16[2,7,128,128]{3,2,1,0:T(8,128)(2,1)} %a_own.1) | copy-start | bytes 1376260
  2.2 26.9 %all-to-all-start = ((s16[16,144,128]{2,1,0:T(8,128)(2,1)}), s16[16,144,128]{2,1,0:T(8,128)(2,1)S(1)}, u32[]{:S(2)}, u32[]{:S(2)}) async-start(s16[16,144,128]{2,1,0:T(8,128)(2,1)} %get-tuple-element.7), calls=%async_computation | async-start | bytes 1179648 | tf_op jit(solution)/shard_map/all_to_all | solution.py:168
  11.6 16.7 %collective-permute-start = (s16[2,144,128]{2,1,0:T(8,128)(2,1)S(1)}, s16[2,144,128]{2,1,0:T(8,128)(2,1)S(1)}, u32[]{:S(2)}, u32[]{:S(2)}) collective-permute-start(s16[2,144,128]{2,1,0:T(8,128)(2,1)S(1)} %copy-done.4), channel_id=1, source_target_pairs={{0,17},{1,16},{2,19},{3,18},{4,21},{5,20},{6,23},{7,22},{8,25},{9,... | collective-permute-start | bytes 221192 | tf_op jit(solution)/shard_map/ppermute | solution.py:167
  22.6 13.9 %collective-permute-start.1 = (bf16[2,7,128,128]{3,2,1,0:T(8,128)(2,1)S(1)}, bf16[2,7,128,128]{3,2,1,0:T(8,128)(2,1)S(1)}, u32[]{:S(2)}, u32[]{:S(2)}) collective-permute-start(bf16[2,7,128,128]{3,2,1,0:T(8,128)(2,1)S(1)} %broadcast_select_fusion), channel_id=1, source_target_pairs={{0,128},{32,160},{64,192},{96,224},{128,0},{160,32},{192,64},{224,... | collective-permute-start | bytes 1376264 | tf_op jit(solution)/shard_map/ppermute | solution.py:166
  29.2 17.7 %copy-start.2 = (s32[64,7]{0,1:T(8,128)S(1)}, s32[64,7]{0,1:T(8,128)}, u32[]{:S(2)}) copy-start(s32[64,7]{0,1:T(8,128)} %param.6) | copy-start | bytes 5380
  29.2 17.7 %copy-start.3 = (s32[64]{0:T(128)S(1)}, s32[64]{0:T(128)}, u32[]{:S(2)}) copy-start(s32[64]{0:T(128)} %aggregates_ref.3) | copy-start | bytes 772
  29.2 17.6 %all-to-all-start.1 = ((s16[16,144,128]{2,1,0:T(8,128)(2,1)}), s16[16,144,128]{2,1,0:T(8,128)(2,1)S(1)}, u32[]{:S(2)}, u32[]{:S(2)}) async-start(s16[16,144,128]{2,1,0:T(8,128)(2,1)} %spread.1), calls=%async_computation.1 | async-start | bytes 1179648 | tf_op jit(solution)/shard_map/all_to_all | solution.py:178
  36.5 10.3 %collective-permute-start.2 = (bf16[2,7,128,128]{3,2,1,0:T(8,128)(2,1)S(1)}, bf16[2,7,128,128]{3,2,1,0:T(8,128)(2,1)S(1)}, u32[]{:S(2)}, u32[]{:S(2)}) collective-permute-start(bf16[2,7,128,128]{3,2,1,0:T(8,128)(2,1)S(1)} %collective-permute-done.1.a_or_p), channel_id=1, source_target_pairs={{0,2},{2,0},{4,6},{6,4},{8,10},{10,8},{12,14},{14,12},{16,18},{18,... | collective-permute-start | bytes 1376264 | tf_op jit(solution)/shard_map/ppermute | solution.py:179
  62.3 11.6 %collective-permute-start.3 = (f32[128,128]{1,0:T(8,128)S(1)}, f32[128,128]{1,0:T(8,128)S(1)}, u32[]{:S(2)}, u32[]{:S(2)}) collective-permute-start(f32[128,128]{1,0:T(8,128)S(1)} %sum.1), channel_id=1, source_target_pairs={{0,16},{1,17},{2,18},{3,19},{4,20},{5,21},{6,22},{7,23},{8,24},{9,... | collective-permute-start | bytes 196616 | tf_op jit(solution)/shard_map/ppermute | solution.py:198
  68.7 10.3 %collective-permute-start.4 = (f32[128,128]{1,0:T(8,128)S(1)}, f32[128,128]{1,0:T(8,128)S(1)}, u32[]{:S(2)}, u32[]{:S(2)}) collective-permute-start(f32[128,128]{1,0:T(8,128)S(1)} %sum.1), channel_id=1, source_target_pairs={{0,17},{1,16},{2,19},{3,18},{4,21},{5,20},{6,23},{7,22},{8,25},{9,... | collective-permute-start | bytes 196616 | tf_op jit(solution)/shard_map/ppermute | solution.py:199

commit v4 on v3

--- a/solution.py
+++ b/solution.py
@@ -41,7 +41,7 @@
     col = lax.axis_index("col")
     start = (lax.axis_index("row") * lax.axis_size("fiber") + lax.axis_index("fiber")) * rows
     low = low_lanes(BLK)
-    wanted = (col, lax.rem(col + ncol // 2, ncol))
+    wanted = (lax.rem(col + ncol // 2, ncol), col)
     sums = [[], []]
     for q in range(rows):
         totals = [jnp.zeros((BLK, BLK), F32) for column in wanted]
@@ -71,26 +71,24 @@
     nfiber = lax.axis_size("fiber")
     fiber = lax.axis_index("fiber")
     row = lax.axis_index("row")
-    low = low_lanes(BLK)
     lane_half = lax.broadcasted_iota(jnp.int32, (1, BLK), 1) // HALF
     total[...] = jnp.zeros_like(total)
     first_core = lax.axis_index("col") % 2 == 0
-    for a_ref, p_ref, panel in ((a_own, p_own, row), (a_or_p, p_or_a, row ^ 4)):
-        paired = a_ref is a_or_p
-
-        def blocks(ref, second_core_ref, q, k):
-            if not paired:
-                return ref[q, k]
-            return jnp.where(first_core, ref[q, k], second_core_ref[q, k])
-
+
+    def own_row(ref, second_core_ref, q):
+        return jnp.concatenate([ref[q, k] for k in range(slots)], axis=1)
+
+    def pair_row(ref, second_core_ref, q):
+        return jnp.concatenate([jnp.where(first_core, ref[q, k], second_core_ref[q, k]) for k in range(slots)], axis=1)
+
+    for a_ref, p_ref, panel, blocks in ((a_own, p_own, row, own_row), (a_or_p, p_or_a, row ^ 4, pair_row)):
         for q in range(rows):
             i = (panel * nfiber + fiber) * rows + q
-            y = jnp.zeros((BLK, 2 * BLK), F32)
+            neighbours = []
             for k in range(slots):
                 j = columns_ref[k, i]
                 source = j // 4
-                layer = (j // 2) % 2
-                near = layer == fiber
+                near = (j // 2) % 2 == fiber
                 block, codes = [
                     jnp.where(near, near_ref[source, part].astype(jnp.int32), far_ref[source, part].astype(jnp.int32))
                     for part in (slice(0, BLK), slice(BLK, BLK + SCALE_ROWS))
@@ -99,34 +97,34 @@
                 block = block.astype(F32) * factor
                 high = block.astype(BF16)
                 rest = (block - high.astype(F32)).astype(BF16)
-                y = y + jnp.dot(blocks(a_ref, p_ref, q, k), jnp.concatenate([high, rest], axis=1), preferred_element_type=F32)
-            y = y[:, :BLK] + y[:, BLK:]
-            y = y + swap_halves(y)
-            high = y.astype(BF16).astype(F32)
-            split = jnp.where(low, high, y - high).astype(BF16)
+                neighbours.append(jnp.concatenate([high, rest], axis=1))
+            y = jnp.dot(
+                blocks(a_ref, p_ref, q), jnp.concatenate(neighbours, axis=0), preferred_element_type=F32
+            )
+            y = (y[:, :BLK] + y[:, BLK:]).T
+            y = y[:HALF] + y[HALF:]
+            high = y.astype(BF16)
+            rest = (y - high.astype(F32)).astype(BF16)
+            lifted = jnp.dot(
+                jnp.concatenate([high, rest], axis=0), blocks(p_ref, a_ref, q), preferred_element_type=F32
+            )
+            lifted = lifted[:HALF] + lifted[HALF:]
             for k in range(slots):
                 group = aggregates_ref[columns_ref[k, i]]
-                lifted = lax.dot_general(blocks(p_ref, a_ref, q, k), split, (((0,), (0,)), ((), ())), preferred_element_type=F32)
-                total[group] += lifted
-    low = low_lanes(HALF)
+                total[group] += lifted[:, k * BLK : (k + 1) * BLK]
     for coarse in range(total.shape[0]):
-        tile = total[coarse]
-        tile = tile + swap_halves(tile)
-        steps, scale = code(jnp.where(low, tile[:HALF], tile[HALF:]))
+        steps, scale = code(total[coarse])
         out_ref[coarse, 0:HALF, :] = steps
         out_ref[coarse, HALF : HALF + SCALE_ROWS, :] = scale
 
 
 def sum_kernel(parts_ref, out_ref):
-    low = low_lanes(HALF)
     halves = [jnp.zeros((HALF, BLK), F32), jnp.zeros((HALF, BLK), F32)]
     for source in range(parts_ref.shape[0]):
         h = (source // 4) % 2
         factor = scale_of(parts_ref[source, HALF : HALF + SCALE_ROWS, :].astype(jnp.int32))
         halves[h] = halves[h] + parts_ref[source, 0:HALF, :].astype(jnp.int32).astype(F32) * factor
-    left, right = halves
-    out_ref[0:HALF, :] = jnp.where(low, left, swap_halves(right))
-    out_ref[HALF:BLK, :] = jnp.where(low, swap_halves(left), right)
+    out_ref[...] = jnp.concatenate(halves, axis=0).T
 
 
 SMEM = pl.BlockSpec(memory_space=pltpu.SMEM)
@@ -182,7 +180,7 @@
         out_shape=jax.ShapeDtypeStruct((nrow, HALF + SCALE_ROWS, BLK), jnp.int16),
         in_specs=[SMEM, SMEM] + [VMEM] * 6,
         out_specs=VMEM,
-        scratch_shapes=[pltpu.VMEM((nrow, BLK, BLK), F32)],
+        scratch_shapes=[pltpu.VMEM((nrow, HALF, BLK), F32)],
         compiler_params=pltpu.CompilerParams(vmem_limit_bytes=16 * 1024 * 1024),
         name="main",
     )(columns, aggregates, near, far, a_blocks, p_terms, from_pair, from_core)
@@ -195,9 +193,8 @@
         compiler_params=pltpu.CompilerParams(vmem_limit_bytes=4 * 1024 * 1024),
         name="sum",
     )(received)
-    up = lax.ppermute(tile, ("col", "fiber"), along(ncol // 4))
-    down = lax.ppermute(tile, ("col", "fiber"), along(-(ncol // 4)))
-    return up + down
+    layers = lax.all_gather(tile, "fiber")
+    return layers[0] + layers[1]
 
 
 def solution(mesh):

time: 80.1 us -> 76.2 us (0.951)
  blocking collectives: 11.9 us -> 25.6 us
  starting transfers between devices: 43.3 us -> 32.9 us
  waiting for transfers between devices: 16.9 us -> 10.6 us
  Pallas kernels: 6.68 us -> 5.76 us
    all_gather x0 -> x1, blocking collectives: none -> 13.7 us  [local(): layers = lax.all_gather(tile, 'fiber')]
    ppermute x2 -> x0, starting transfers between devices: 10.4 us -> none  [the longest x1 6.38 us: local(): up = lax.ppermute(tile, ('col', 'fiber'), along(ncol // 4))]
    ppermute x2 -> x0, waiting for transfers between devices: 6.27 us -> none  [the longest x1 5.04 us: local(): down = lax.ppermute(tile, ('col', 'fiber'), along(-(ncol // 4)))]
    pallas_call x1, Pallas kernels: 3.39 us -> 2.48 us  [local(): pl.pallas_call(main_kernel, out_shape=jax.ShapeDtypeStruct((nrow, HALF +...]
  transfers between devices with their start and end apart: 7 -> 5, of which waited for: 4 -> 2; matrix products, arithmetic and copies ran while one was open for 0% -> 0% of each run, Pallas kernels for 1% -> 1%
where the time goes in v4:
time: 76.2 us; the launch traced here: 75.7 us
  starting transfers between devices  32.9 us (43%)
  blocking collectives  25.6 us (34%)
  waiting for transfers between devices  10.6 us (14%)
  Pallas kernels  5.76 us (8%)
    all_gather x1, blocking collectives, local(): layers = lax.all_gather(tile, 'fiber')  13.7 us
    all_to_all x1, blocking collectives, local(): received = lax.all_to_all(parts, 'row', 0, 0, tiled=True)  11.9 us
    ppermute x1, starting transfers between devices, local(): crossed = lax.ppermute(partner, ('col', 'fiber'), across)  10.9 us
    all_to_all x1, starting transfers between devices, local(): near = lax.all_to_all(own, 'row', 0, 0, tiled=True)  9.34 us
    all_to_all x1, waiting for transfers between devices, local(): far = lax.all_to_all(spread, 'row', 0, 0, tiled=True)  8.35 us
    all_to_all x1, starting transfers between devices, local(): far = lax.all_to_all(spread, 'row', 0, 0, tiled=True)  7.36 us
    ppermute x1, starting transfers between devices, local(): from_pair = lax.ppermute(here, 'row', pairs)  3.37 us
    pallas_call x1, Pallas kernels, local(): pl.pallas_call(main_kernel, out_shape=jax.ShapeDtypeStruct((nrow, HALF +...  2.48 us
  transfers between devices with their start and end apart: 5, of which 2 were waited for; matrix products, arithmetic and copies ran while one was open for 0% of the time, Pallas kernels for 1%

profile of v4, /device:TPU:8, one launch (start us, length us, event | category | flops | bytes accessed | tf_op | source)
XLA Modules:
  0.0 75.7 jit_solution(10504039819410464611)
XLA Ops:
  0.0 2.2 %build.1 = (s16[2,144,128]{2,1,0:T(8,128)(2,1)}, s16[16,144,128]{2,1,0:T(8,128)(2,1)}) custom-call(s32[7,64]{1,0:T(8,128)} %bitcast.1, s32[64]{0:T(128)} %aggregates_ref.3, bf16[2,7,128,128]{3,2,1,0:T(8,128)(2,1)} %p_own.1), custom_call_target="tpu_custom_call" | custom-call | tf_op jit(solution)/shard_map/build/pallas_call | solution.py:153
  2.2 0.0 copy-start.4
  2.2 0.0 copy-start
  2.2 0.0 copy-start.1
  2.2 9.3 %all-to-all-start = ((s16[16,144,128]{2,1,0:T(8,128)(2,1)}), s16[16,144,128]{2,1,0:T(8,128)(2,1)S(1)}, u32[]{:S(2)}, u32[]{:S(2)}) async-start(s16[16,144,128]{2,1,0:T(8,128)(2,1)} %get-tuple-element.7), calls=%async_computation | async-start | bytes 1179648 | tf_op jit(solution)/shard_map/all_to_all | solution.py:166
  11.6 0.0 copy-done.4
  11.6 10.9 %collective-permute-start = (s16[2,144,128]{2,1,0:T(8,128)(2,1)S(1)}, s16[2,144,128]{2,1,0:T(8,128)(2,1)S(1)}, u32[]{:S(2)}, u32[]{:S(2)}) collective-permute-start(s16[2,144,128]{2,1,0:T(8,128)(2,1)S(1)} %copy-done.4), channel_id=1, source_target_pairs={{0,17},{1,16},{2,19},{3,18},{4,21},{5,20},{6,23},{7,22},{8,25},{9,... | collective-permute-start | bytes 221192 | tf_op jit(solution)/shard_map/ppermute | solution.py:165
  22.5 0.0 copy-done
  22.6 0.0 copy-done.1
  22.6 0.1 broadcast_select_fusion
  22.6 3.4 %collective-permute-start.1 = (bf16[2,7,128,128]{3,2,1,0:T(8,128)(2,1)S(1)}, bf16[2,7,128,128]{3,2,1,0:T(8,128)(2,1)S(1)}, u32[]{:S(2)}, u32[]{:S(2)}) collective-permute-start(bf16[2,7,128,128]{3,2,1,0:T(8,128)(2,1)S(1)} %broadcast_select_fusion), channel_id=1, source_target_pairs={{0,128},{32,160},{64,192},{96,224},{128,0},{160,32},{192,64},{224,... | collective-permute-start | bytes 1376264 | tf_op jit(solution)/shard_map/ppermute | solution.py:164
  26.0 2.2 %collective-permute-done.pair_ref = s16[2,144,128]{2,1,0:T(8,128)(2,1)S(1)} collective-permute-done((s16[2,144,128]{2,1,0:T(8,128)(2,1)S(1)}, s16[2,144,128]{2,1,0:T(8,128)(2,1)S(1)}, u32[]{:S(2)}, u32[]{:S(2)}) %collective-permute-start) | collective-permute-done | bytes 73760 | tf_op jit(solution)/shard_map/ppermute | solution.py:165
  28.2 0.9 %spread.1 = s16[16,144,128]{2,1,0:T(8,128)(2,1)} custom-call(s16[2,144,128]{2,1,0:T(8,128)(2,1)S(1)} %collective-permute-done.pair_ref), custom_call_target="tpu_custom_call" | custom-call | flops 137438953472 | bytes 2097152 | tf_op jit(solution)/shard_map/spread/pallas_call | solution.py:167
  29.1 0.0 copy-start.2
  29.1 0.0 copy-start.3
  29.1 0.0 all-to-all-done.near_ref
  29.1 7.4 %all-to-all-start.1 = ((s16[16,144,128]{2,1,0:T(8,128)(2,1)}), s16[16,144,128]{2,1,0:T(8,128)(2,1)S(1)}, u32[]{:S(2)}, u32[]{:S(2)}) async-start(s16[16,144,128]{2,1,0:T(8,128)(2,1)} %spread.1), calls=%async_computation.1 | async-start | bytes 1179648 | tf_op jit(solution)/shard_map/all_to_all | solution.py:176
  36.5 0.0 collective-permute-done.1.a_or_p
  36.5 1.9 %collective-permute-start.2 = (bf16[2,7,128,128]{3,2,1,0:T(8,128)(2,1)S(1)}, bf16[2,7,128,128]{3,2,1,0:T(8,128)(2,1)S(1)}, u32[]{:S(2)}, u32[]{:S(2)}) collective-permute-start(bf16[2,7,128,128]{3,2,1,0:T(8,128)(2,1)S(1)} %collective-permute-done.1.a_or_p), channel_id=1, source_target_pairs={{0,2},{2,0},{4,6},{6,4},{8,10},{10,8},{12,14},{14,12},{16,18},{18,... | collective-permute-start | bytes 1376264 | tf_op jit(solution)/shard_map/ppermute | solution.py:177
  38.4 8.4 %all-to-all-done.1.far_ref = s16[16,144,128]{2,1,0:T(8,128)(2,1)S(1)} async-done(((s16[16,144,128]{2,1,0:T(8,128)(2,1)}), s16[16,144,128]{2,1,0:T(8,128)(2,1)S(1)}, u32[]{:S(2)}, u32[]{:S(2)}) %all-to-all-start.1) | async-done | bytes 589856 | tf_op jit(solution)/shard_map/all_to_all | solution.py:176
  46.8 0.0 collective-permute-done.2.p_or_a
  46.8 0.0 copy-done.2
  46.8 0.0 copy-done.3
  46.8 2.5 %main.1 = s16[16,80,128]{2,1,0:T(8,128)(2,1)S(1)} custom-call(s32[7,64]{1,0:T(8,128)S(1)} %bitcast.2, s32[64]{0:T(128)S(1)} %copy-done.3, s16[16,144,128]{2,1,0:T(8,128)(2,1)S(1)} %all-to-all-done.near_ref, s16[16,144,128]{2,1,0:T(8,128)(2,1)S(1)} %all-to-all-done.1.far_ref, bf16[2,7,128,128]{3,2,1,0:T(8,128)(2,1)S(1)} %copy-done.1, ...), custom_call_target="tpu_custom_call" | custom-call | tf_op jit(solution)/shard_map/main/pallas_call | solution.py:178
  49.3 11.9 %all_to_all.15.parts_ref = s16[16,80,128]{2,1,0:T(8,128)(2,1)S(1)} all-to-all(s16[16,80,128]{2,1,0:T(8,128)(2,1)S(1)} %main.1), channel_id=1, replica_groups=mesh['row'=16,'col'=16,'fiber'=2] {'row'}, dimensions={0} | all-to-all | bytes 655360 | tf_op jit(solution)/shard_map/all_to_all | solution.py:187
  61.2 0.2 sum.1
  61.4 13.7 %all-gather = f32[256,128]{1,0:T(8,128)S(1)} all-gather(f32[128,128]{1,0:T(8,128)S(1)} %sum.1), channel_id=2, replica_groups=mesh['row'=16,'col'=16,'fiber'=2] {'fiber'}, dimensions={0}, use_global_device_ids=true | all-gather | bytes 196608 | tf_op jit(solution)/shard_map/all_gather | solution.py:196
  75.1 0.6 slice_add_fusion
Async XLA Ops:
  2.2 9.3 %copy-start.4 = (s16[2,144,128]{2,1,0:T(8,128)(2,1)S(1)}, s16[2,144,128]{2,1,0:T(8,128)(2,1)}, u32[]{:S(2)}) copy-start(s16[2,144,128]{2,1,0:T(8,128)(2,1)} %get-tuple-element.8) | copy-start | bytes 221188
  2.2 20.3 %copy-start = (bf16[2,7,128,128]{3,2,1,0:T(8,128)(2,1)S(1)}, bf16[2,7,128,128]{3,2,1,0:T(8,128)(2,1)}, u32[]{:S(2)}) copy-start(bf16[2,7,128,128]{3,2,1,0:T(8,128)(2,1)} %p_own.1) | copy-start | bytes 1376260
  2.2 20.3 %copy-start.1 = (bf16[2,7,128,128]{3,2,1,0:T(8,128)(2,1)S(1)}, bf16[2,7,128,128]{3,2,1,0:T(8,128)(2,1)}, u32[]{:S(2)}) copy-start(bf16[2,7,128,128]{3,2,1,0:T(8,128)(2,1)} %a_own.1) | copy-start | bytes 1376260
  2.2 26.9 %all-to-all-start = ((s16[16,144,128]{2,1,0:T(8,128)(2,1)}), s16[16,144,128]{2,1,0:T(8,128)(2,1)S(1)}, u32[]{:S(2)}, u32[]{:S(2)}) async-start(s16[16,144,128]{2,1,0:T(8,128)(2,1)} %get-tuple-element.7), calls=%async_computation | async-start | bytes 1179648 | tf_op jit(solution)/shard_map/all_to_all | solution.py:166
  11.6 16.7 %collective-permute-start = (s16[2,144,128]{2,1,0:T(8,128)(2,1)S(1)}, s16[2,144,128]{2,1,0:T(8,128)(2,1)S(1)}, u32[]{:S(2)}, u32[]{:S(2)}) collective-permute-start(s16[2,144,128]{2,1,0:T(8,128)(2,1)S(1)} %copy-done.4), channel_id=1, source_target_pairs={{0,17},{1,16},{2,19},{3,18},{4,21},{5,20},{6,23},{7,22},{8,25},{9,... | collective-permute-start | bytes 221192 | tf_op jit(solution)/shard_map/ppermute | solution.py:165
  22.6 13.9 %collective-permute-start.1 = (bf16[2,7,128,128]{3,2,1,0:T(8,128)(2,1)S(1)}, bf16[2,7,128,128]{3,2,1,0:T(8,128)(2,1)S(1)}, u32[]{:S(2)}, u32[]{:S(2)}) collective-permute-start(bf16[2,7,128,128]{3,2,1,0:T(8,128)(2,1)S(1)} %broadcast_select_fusion), channel_id=1, source_target_pairs={{0,128},{32,160},{64,192},{96,224},{128,0},{160,32},{192,64},{224,... | collective-permute-start | bytes 1376264 | tf_op jit(solution)/shard_map/ppermute | solution.py:164
  29.1 17.7 %copy-start.2 = (s32[64,7]{0,1:T(8,128)S(1)}, s32[64,7]{0,1:T(8,128)}, u32[]{:S(2)}) copy-start(s32[64,7]{0,1:T(8,128)} %param.6) | copy-start | bytes 5380
  29.1 17.7 %copy-start.3 = (s32[64]{0:T(128)S(1)}, s32[64]{0:T(128)}, u32[]{:S(2)}) copy-start(s32[64]{0:T(128)} %aggregates_ref.3) | copy-start | bytes 772
  29.1 17.6 %all-to-all-start.1 = ((s16[16,144,128]{2,1,0:T(8,128)(2,1)}), s16[16,144,128]{2,1,0:T(8,128)(2,1)S(1)}, u32[]{:S(2)}, u32[]{:S(2)}) async-start(s16[16,144,128]{2,1,0:T(8,128)(2,1)} %spread.1), calls=%async_computation.1 | async-start | bytes 1179648 | tf_op jit(solution)/shard_map/all_to_all | solution.py:176
  36.5 10.3 %collective-permute-start.2 = (bf16[2,7,128,128]{3,2,1,0:T(8,128)(2,1)S(1)}, bf16[2,7,128,128]{3,2,1,0:T(8,128)(2,1)S(1)}, u32[]{:S(2)}, u32[]{:S(2)}) collective-permute-start(bf16[2,7,128,128]{3,2,1,0:T(8,128)(2,1)S(1)} %collective-permute-done.1.a_or_p), channel_id=1, source_target_pairs={{0,2},{2,0},{4,6},{6,4},{8,10},{10,8},{12,14},{14,12},{16,18},{18,... | collective-permute-start | bytes 1376264 | tf_op jit(solution)/shard_map/ppermute | solution.py:177

commit v5 on v4

--- a/solution.py
+++ b/solution.py
@@ -18,21 +18,13 @@
     largest = jnp.max(jnp.abs(value), axis=0, keepdims=True)
     exponent = jnp.ceil(jnp.log2(jnp.maximum(largest, 2.0**-111)) * STEPS)
     steps = jnp.floor(value * (jnp.exp2(exponent * (-1.0 / STEPS)) * TOP) + 0.5)
-    scale = jnp.broadcast_to(exponent, (SCALE_ROWS, value.shape[1]))
-    return steps.astype(jnp.int32).astype(jnp.int16), scale.astype(jnp.int32).astype(jnp.int16)
+    scale = jnp.broadcast_to(exponent, (SCALE_ROWS // 2, value.shape[1]))
+    return steps.astype(jnp.int32), scale.astype(jnp.int32)
 
 
 def scale_of(codes):
     exponent = codes[0:1].astype(F32)
     return jnp.exp2(exponent * (1.0 / STEPS)) * (1.0 / TOP)
-
-
-def low_lanes(rows):
-    return lax.broadcasted_iota(jnp.int32, (rows, BLK), 1) < HALF
-
-
-def swap_halves(value):
-    return pltpu.roll(value, HALF, 1)
 
 
 def build_kernel(columns_ref, aggregates_ref, terms_ref, partner_ref, own_ref):
@@ -40,7 +32,6 @@
     ncol = lax.axis_size("col")
     col = lax.axis_index("col")
     start = (lax.axis_index("row") * lax.axis_size("fiber") + lax.axis_index("fiber")) * rows
-    low = low_lanes(BLK)
     wanted = (lax.rem(col + ncol // 2, ncol), col)
     sums = [[], []]
     for q in range(rows):
@@ -51,14 +42,15 @@
             totals = [t + term * jnp.where(group == column, 1.0, 0.0) for t, column in zip(totals, wanted)]
         for side, total in zip(sums, totals):
             side.append(total)
-    for out_ref, (p0, p1) in zip((partner_ref, own_ref), sums):
-        packed = (jnp.where(low, p0, swap_halves(p1)), jnp.where(low, swap_halves(p0), p1))
+    for out_ref, blocks in zip((partner_ref, own_ref), sums):
+        blocks = [block.T for block in blocks]
         for h in range(2):
-            steps, scale = code(packed[h])
+            steps, scales = zip(*[code(block[h * HALF : (h + 1) * HALF]) for block in blocks])
+            steps, scales = jnp.concatenate(steps, axis=0), jnp.concatenate(scales, axis=0)
             for target in range(out_ref.shape[0]):
                 if out_ref is partner_ref and target == h or out_ref is own_ref and target // 4 % 2 == h:
-                    out_ref[target, 0:BLK, :] = steps
-                    out_ref[target, BLK : BLK + SCALE_ROWS, :] = scale
+                    out_ref[target, 0:BLK, :] = steps.astype(jnp.int16)
+                    out_ref[target, BLK : BLK + SCALE_ROWS, :] = scales.astype(jnp.int16)
 
 
 def spread_kernel(pair_ref, out_ref):
@@ -71,7 +63,6 @@
     nfiber = lax.axis_size("fiber")
     fiber = lax.axis_index("fiber")
     row = lax.axis_index("row")
-    lane_half = lax.broadcasted_iota(jnp.int32, (1, BLK), 1) // HALF
     total[...] = jnp.zeros_like(total)
     first_core = lax.axis_index("col") % 2 == 0
 
@@ -81,41 +72,48 @@
     def pair_row(ref, second_core_ref, q):
         return jnp.concatenate([jnp.where(first_core, ref[q, k], second_core_ref[q, k]) for k in range(slots)], axis=1)
 
-    for a_ref, p_ref, panel, blocks in ((a_own, p_own, row, own_row), (a_or_p, p_or_a, row ^ 4, pair_row)):
-        for q in range(rows):
-            i = (panel * nfiber + fiber) * rows + q
-            neighbours = []
-            for k in range(slots):
-                j = columns_ref[k, i]
-                source = j // 4
-                near = (j // 2) % 2 == fiber
-                block, codes = [
-                    jnp.where(near, near_ref[source, part].astype(jnp.int32), far_ref[source, part].astype(jnp.int32))
-                    for part in (slice(0, BLK), slice(BLK, BLK + SCALE_ROWS))
-                ]
-                factor = jnp.where(lane_half == j % 2, scale_of(codes), 0.0)
-                block = block.astype(F32) * factor
-                high = block.astype(BF16)
-                rest = (block - high.astype(F32)).astype(BF16)
-                neighbours.append(jnp.concatenate([high, rest], axis=1))
-            y = jnp.dot(
-                blocks(a_ref, p_ref, q), jnp.concatenate(neighbours, axis=0), preferred_element_type=F32
+    sides = ((a_own, p_own, row, own_row), (a_or_p, p_or_a, row ^ 4, pair_row))
+    fine = [(*side, q, (side[2] * nfiber + fiber) * rows + q) for side in sides for q in range(rows)]
+    products = []
+    for a_ref, p_ref, panel, blocks, q, i in fine:
+        neighbours = []
+        for k in range(slots):
+            j = columns_ref[k, i]
+            source = j // 4
+            near = (j // 2) % 2 == fiber
+            place = pl.ds(pl.multiple_of(j % 2 * HALF, HALF), HALF)
+            block, codes = [
+                jnp.where(near, near_ref[source, part].astype(jnp.int32), far_ref[source, part].astype(jnp.int32))
+                for part in (place, slice(BLK, BLK + SCALE_ROWS))
+            ]
+            codes = jnp.where(j % 2 == 0, codes[0:1], codes[SCALE_ROWS // 2 : SCALE_ROWS // 2 + 1])
+            block = block.astype(F32) * scale_of(codes)
+            high = block.astype(BF16)
+            rest = (block - high.astype(F32)).astype(BF16)
+            neighbours.append(jnp.concatenate([high, rest], axis=0))
+        products.append(
+            lax.dot_general(
+                jnp.concatenate(neighbours, axis=1),
+                blocks(a_ref, p_ref, q),
+                (((1,), (1,)), ((), ())),
+                preferred_element_type=F32,
             )
-            y = (y[:, :BLK] + y[:, BLK:]).T
-            y = y[:HALF] + y[HALF:]
-            high = y.astype(BF16)
-            rest = (y - high.astype(F32)).astype(BF16)
-            lifted = jnp.dot(
-                jnp.concatenate([high, rest], axis=0), blocks(p_ref, a_ref, q), preferred_element_type=F32
-            )
-            lifted = lifted[:HALF] + lifted[HALF:]
-            for k in range(slots):
-                group = aggregates_ref[columns_ref[k, i]]
-                total[group] += lifted[:, k * BLK : (k + 1) * BLK]
+        )
+    lifted = []
+    for (a_ref, p_ref, panel, blocks, q, i), y in zip(fine, products):
+        y = y[:HALF] + y[HALF:]
+        high = y.astype(BF16)
+        rest = (y - high.astype(F32)).astype(BF16)
+        both = jnp.dot(jnp.concatenate([high, rest], axis=0), blocks(p_ref, a_ref, q), preferred_element_type=F32)
+        lifted.append(both[:HALF] + both[HALF:])
+    for (a_ref, p_ref, panel, blocks, q, i), part in zip(fine, lifted):
+        for k in range(slots):
+            group = aggregates_ref[columns_ref[k, i]]
+            total[group] += part[:, k * BLK : (k + 1) * BLK]
     for coarse in range(total.shape[0]):
         steps, scale = code(total[coarse])
-        out_ref[coarse, 0:HALF, :] = steps
-        out_ref[coarse, HALF : HALF + SCALE_ROWS, :] = scale
+        out_ref[coarse, 0:HALF, :] = steps.astype(jnp.int16)
+        out_ref[coarse, HALF : HALF + SCALE_ROWS, :] = jnp.concatenate([scale, scale], axis=0).astype(jnp.int16)
 
 
 def sum_kernel(parts_ref, out_ref):
@@ -124,7 +122,17 @@
         h = (source // 4) % 2
         factor = scale_of(parts_ref[source, HALF : HALF + SCALE_ROWS, :].astype(jnp.int32))
         halves[h] = halves[h] + parts_ref[source, 0:HALF, :].astype(jnp.int32).astype(F32) * factor
-    out_ref[...] = jnp.concatenate(halves, axis=0).T
+    steps, scale = code(jnp.concatenate(halves, axis=0).T)
+    out_ref[0:BLK, :] = steps.astype(jnp.int16)
+    out_ref[BLK : BLK + SCALE_ROWS, :] = jnp.concatenate([scale, scale], axis=0).astype(jnp.int16)
+
+
+def add_kernel(layers_ref, out_ref):
+    total = jnp.zeros_like(out_ref)
+    for layer in range(layers_ref.shape[0]):
+        factor = scale_of(layers_ref[layer, BLK : BLK + SCALE_ROWS, :].astype(jnp.int32))
+        total = total + layers_ref[layer, 0:BLK, :].astype(jnp.int32).astype(F32) * factor
+    out_ref[...] = total
 
 
 SMEM = pl.BlockSpec(memory_space=pltpu.SMEM)
@@ -187,14 +195,21 @@
     received = lax.all_to_all(parts, "row", 0, 0, tiled=True)
     tile = pl.pallas_call(
         sum_kernel,
-        out_shape=jax.ShapeDtypeStruct((BLK, BLK), F32),
+        out_shape=jax.ShapeDtypeStruct((packed_rows, BLK), jnp.int16),
         in_specs=[VMEM],
         out_specs=VMEM,
         compiler_params=pltpu.CompilerParams(vmem_limit_bytes=4 * 1024 * 1024),
         name="sum",
     )(received)
     layers = lax.all_gather(tile, "fiber")
-    return layers[0] + layers[1]
+    return pl.pallas_call(
+        add_kernel,
+        out_shape=jax.ShapeDtypeStruct((BLK, BLK), F32),
+        in_specs=[VMEM],
+        out_specs=VMEM,
+        compiler_params=pltpu.CompilerParams(vmem_limit_bytes=4 * 1024 * 1024),
+        name="add",
+    )(layers)
 
 
 def solution(mesh):

time: 76.2 us -> 75.1 us (0.986)
  no operation moved by 1% of the time
where the time goes in v5:
time: 75.1 us; the launch traced here: 74.7 us
  starting transfers between devices  32.9 us (44%)
  blocking collectives  25.3 us (34%)
  waiting for transfers between devices  10.6 us (14%)
  Pallas kernels  5.67 us (8%)
    all_gather x1, blocking collectives, local(): layers = lax.all_gather(tile, 'fiber')  13.3 us
    all_to_all x1, blocking collectives, local(): received = lax.all_to_all(parts, 'row', 0, 0, tiled=True)  12 us
    ppermute x1, starting transfers between devices, local(): crossed = lax.ppermute(partner, ('col', 'fiber'), across)  10.9 us
    all_to_all x1, starting transfers between devices, local(): near = lax.all_to_all(own, 'row', 0, 0, tiled=True)  9.34 us
    all_to_all x1, waiting for transfers between devices, local(): far = lax.all_to_all(spread, 'row', 0, 0, tiled=True)  8.35 us
    all_to_all x1, starting transfers between devices, local(): far = lax.all_to_all(spread, 'row', 0, 0, tiled=True)  7.36 us
    ppermute x1, starting transfers between devices, local(): from_pair = lax.ppermute(here, 'row', pairs)  3.37 us
    ppermute x1, waiting for transfers between devices, local(): crossed = lax.ppermute(partner, ('col', 'fiber'), across)  2.25 us
  transfers between devices with their start and end apart: 5, of which 2 were waited for; matrix products, arithmetic and copies ran while one was open for 0% of the time, Pallas kernels for 1%

profile of v5, /device:TPU:8, one launch (start us, length us, event | category | flops | bytes accessed | tf_op | source)
XLA Modules:
  0.0 74.7 jit_solution(3194996590548072028)
XLA Ops:
  0.0 2.2 %build.1 = (s16[2,144,128]{2,1,0:T(8,128)(2,1)}, s16[16,144,128]{2,1,0:T(8,128)(2,1)}) custom-call(s32[7,64]{1,0:T(8,128)} %bitcast.3, s32[64]{0:T(128)} %aggregates_ref.3, bf16[2,7,128,128]{3,2,1,0:T(8,128)(2,1)} %p_own.1), custom_call_target="tpu_custom_call" | custom-call | tf_op jit(solution)/shard_map/build/pallas_call | solution.py:161
  2.2 0.0 copy-start.4
  2.2 0.0 copy-start
  2.2 0.0 copy-start.1
  2.2 9.3 %all-to-all-start = ((s16[16,144,128]{2,1,0:T(8,128)(2,1)}), s16[16,144,128]{2,1,0:T(8,128)(2,1)S(1)}, u32[]{:S(2)}, u32[]{:S(2)}) async-start(s16[16,144,128]{2,1,0:T(8,128)(2,1)} %get-tuple-element.7), calls=%async_computation | async-start | bytes 1179648 | tf_op jit(solution)/shard_map/all_to_all | solution.py:174
  11.6 0.0 copy-done.4
  11.6 10.9 %collective-permute-start = (s16[2,144,128]{2,1,0:T(8,128)(2,1)S(1)}, s16[2,144,128]{2,1,0:T(8,128)(2,1)S(1)}, u32[]{:S(2)}, u32[]{:S(2)}) collective-permute-start(s16[2,144,128]{2,1,0:T(8,128)(2,1)S(1)} %copy-done.4), channel_id=1, source_target_pairs={{0,17},{1,16},{2,19},{3,18},{4,21},{5,20},{6,23},{7,22},{8,25},{9,... | collective-permute-start | bytes 221192 | tf_op jit(solution)/shard_map/ppermute | solution.py:173
  22.5 0.0 copy-done
  22.5 0.0 copy-done.1
  22.5 0.1 broadcast_select_fusion
  22.6 3.4 %collective-permute-start.1 = (bf16[2,7,128,128]{3,2,1,0:T(8,128)(2,1)S(1)}, bf16[2,7,128,128]{3,2,1,0:T(8,128)(2,1)S(1)}, u32[]{:S(2)}, u32[]{:S(2)}) collective-permute-start(bf16[2,7,128,128]{3,2,1,0:T(8,128)(2,1)S(1)} %broadcast_select_fusion), channel_id=1, source_target_pairs={{0,128},{32,160},{64,192},{96,224},{128,0},{160,32},{192,64},{224,... | collective-permute-start | bytes 1376264 | tf_op jit(solution)/shard_map/ppermute | solution.py:172
  26.0 2.2 %collective-permute-done.pair_ref = s16[2,144,128]{2,1,0:T(8,128)(2,1)S(1)} collective-permute-done((s16[2,144,128]{2,1,0:T(8,128)(2,1)S(1)}, s16[2,144,128]{2,1,0:T(8,128)(2,1)S(1)}, u32[]{:S(2)}, u32[]{:S(2)}) %collective-permute-start) | collective-permute-done | bytes 73760 | tf_op jit(solution)/shard_map/ppermute | solution.py:173
  28.2 0.9 %spread.1 = s16[16,144,128]{2,1,0:T(8,128)(2,1)} custom-call(s16[2,144,128]{2,1,0:T(8,128)(2,1)S(1)} %collective-permute-done.pair_ref), custom_call_target="tpu_custom_call" | custom-call | flops 137438953472 | bytes 2097152 | tf_op jit(solution)/shard_map/spread/pallas_call | solution.py:175
  29.1 0.0 copy-start.2
  29.1 0.0 copy-start.3
  29.1 0.0 all-to-all-done.near_ref
  29.1 7.4 %all-to-all-start.1 = ((s16[16,144,128]{2,1,0:T(8,128)(2,1)}), s16[16,144,128]{2,1,0:T(8,128)(2,1)S(1)}, u32[]{:S(2)}, u32[]{:S(2)}) async-start(s16[16,144,128]{2,1,0:T(8,128)(2,1)} %spread.1), calls=%async_computation.1 | async-start | bytes 1179648 | tf_op jit(solution)/shard_map/all_to_all | solution.py:184
  36.5 0.0 collective-permute-done.1.a_or_p
  36.5 1.9 %collective-permute-start.2 = (bf16[2,7,128,128]{3,2,1,0:T(8,128)(2,1)S(1)}, bf16[2,7,128,128]{3,2,1,0:T(8,128)(2,1)S(1)}, u32[]{:S(2)}, u32[]{:S(2)}) collective-permute-start(bf16[2,7,128,128]{3,2,1,0:T(8,128)(2,1)S(1)} %collective-permute-done.1.a_or_p), channel_id=1, source_target_pairs={{0,2},{2,0},{4,6},{6,4},{8,10},{10,8},{12,14},{14,12},{16,18},{18,... | collective-permute-start | bytes 1376264 | tf_op jit(solution)/shard_map/ppermute | solution.py:185
  38.4 8.4 %all-to-all-done.1.far_ref = s16[16,144,128]{2,1,0:T(8,128)(2,1)S(1)} async-done(((s16[16,144,128]{2,1,0:T(8,128)(2,1)}), s16[16,144,128]{2,1,0:T(8,128)(2,1)S(1)}, u32[]{:S(2)}, u32[]{:S(2)}) %all-to-all-start.1) | async-done | bytes 589856 | tf_op jit(solution)/shard_map/all_to_all | solution.py:184
  46.8 0.0 collective-permute-done.2.p_or_a
  46.8 0.0 copy-done.2
  46.8 0.0 copy-done.3
  46.8 1.7 %main.1 = s16[16,80,128]{2,1,0:T(8,128)(2,1)S(1)} custom-call(s32[7,64]{1,0:T(8,128)S(1)} %bitcast.4, s32[64]{0:T(128)S(1)} %copy-done.3, s16[16,144,128]{2,1,0:T(8,128)(2,1)S(1)} %all-to-all-done.near_ref, s16[16,144,128]{2,1,0:T(8,128)(2,1)S(1)} %all-to-all-done.1.far_ref, bf16[2,7,128,128]{3,2,1,0:T(8,128)(2,1)S(1)} %copy-done.1, ...), custom_call_target="tpu_custom_call" | custom-call | tf_op jit(solution)/shard_map/main/pallas_call | solution.py:186
  48.5 12.0 %all_to_all.15.parts_ref = s16[16,80,128]{2,1,0:T(8,128)(2,1)S(1)} all-to-all(s16[16,80,128]{2,1,0:T(8,128)(2,1)S(1)} %main.1), channel_id=1, replica_groups=mesh['row'=16,'col'=16,'fiber'=2] {'row'}, dimensions={0} | all-to-all | bytes 655360 | tf_op jit(solution)/shard_map/all_to_all | solution.py:195
  60.5 0.2 sum.1
  60.7 13.3 %all-gather = s16[288,128]{1,0:T(8,128)(2,1)S(1)} all-gather(s16[144,128]{1,0:T(8,128)(2,1)S(1)} %sum.1), channel_id=2, replica_groups=mesh['row'=16,'col'=16,'fiber'=2] {'fiber'}, dimensions={0}, use_global_device_ids=true | all-gather | bytes 110592 | tf_op jit(solution)/shard_map/all_gather | solution.py:204
  74.0 0.6 add.6
Async XLA Ops:
  2.2 9.3 %copy-start.4 = (s16[2,144,128]{2,1,0:T(8,128)(2,1)S(1)}, s16[2,144,128]{2,1,0:T(8,128)(2,1)}, u32[]{:S(2)}) copy-start(s16[2,144,128]{2,1,0:T(8,128)(2,1)} %get-tuple-element.8) | copy-start | bytes 221188
  2.2 20.3 %copy-start = (bf16[2,7,128,128]{3,2,1,0:T(8,128)(2,1)S(1)}, bf16[2,7,128,128]{3,2,1,0:T(8,128)(2,1)}, u32[]{:S(2)}) copy-start(bf16[2,7,128,128]{3,2,1,0:T(8,128)(2,1)} %p_own.1) | copy-start | bytes 1376260
  2.2 20.3 %copy-start.1 = (bf16[2,7,128,128]{3,2,1,0:T(8,128)(2,1)S(1)}, bf16[2,7,128,128]{3,2,1,0:T(8,128)(2,1)}, u32[]{:S(2)}) copy-start(bf16[2,7,128,128]{3,2,1,0:T(8,128)(2,1)} %a_own.1) | copy-start | bytes 1376260
  2.2 26.9 %all-to-all-start = ((s16[16,144,128]{2,1,0:T(8,128)(2,1)}), s16[16,144,128]{2,1,0:T(8,128)(2,1)S(1)}, u32[]{:S(2)}, u32[]{:S(2)}) async-start(s16[16,144,128]{2,1,0:T(8,128)(2,1)} %get-tuple-element.7), calls=%async_computation | async-start | bytes 1179648 | tf_op jit(solution)/shard_map/all_to_all | solution.py:174
  11.6 16.7 %collective-permute-start = (s16[2,144,128]{2,1,0:T(8,128)(2,1)S(1)}, s16[2,144,128]{2,1,0:T(8,128)(2,1)S(1)}, u32[]{:S(2)}, u32[]{:S(2)}) collective-permute-start(s16[2,144,128]{2,1,0:T(8,128)(2,1)S(1)} %copy-done.4), channel_id=1, source_target_pairs={{0,17},{1,16},{2,19},{3,18},{4,21},{5,20},{6,23},{7,22},{8,25},{9,... | collective-permute-start | bytes 221192 | tf_op jit(solution)/shard_map/ppermute | solution.py:173
  22.6 13.9 %collective-permute-start.1 = (bf16[2,7,128,128]{3,2,1,0:T(8,128)(2,1)S(1)}, bf16[2,7,128,128]{3,2,1,0:T(8,128)(2,1)S(1)}, u32[]{:S(2)}, u32[]{:S(2)}) collective-permute-start(bf16[2,7,128,128]{3,2,1,0:T(8,128)(2,1)S(1)} %broadcast_select_fusion), channel_id=1, source_target_pairs={{0,128},{32,160},{64,192},{96,224},{128,0},{160,32},{192,64},{224,... | collective-permute-start | bytes 1376264 | tf_op jit(solution)/shard_map/ppermute | solution.py:172
  29.1 17.7 %copy-start.2 = (s32[64,7]{0,1:T(8,128)S(1)}, s32[64,7]{0,1:T(8,128)}, u32[]{:S(2)}) copy-start(s32[64,7]{0,1:T(8,128)} %param.6) | copy-start | bytes 5380
  29.1 17.7 %copy-start.3 = (s32[64]{0:T(128)S(1)}, s32[64]{0:T(128)}, u32[]{:S(2)}) copy-start(s32[64]{0:T(128)} %aggregates_ref.3) | copy-start | bytes 772
  29.1 17.6 %all-to-all-start.1 = ((s16[16,144,128]{2,1,0:T(8,128)(2,1)}), s16[16,144,128]{2,1,0:T(8,128)(2,1)S(1)}, u32[]{:S(2)}, u32[]{:S(2)}) async-start(s16[16,144,128]{2,1,0:T(8,128)(2,1)} %spread.1), calls=%async_computation.1 | async-start | bytes 1179648 | tf_op jit(solution)/shard_map/all_to_all | solution.py:184
  36.5 10.3 %collective-permute-start.2 = (bf16[2,7,128,128]{3,2,1,0:T(8,128)(2,1)S(1)}, bf16[2,7,128,128]{3,2,1,0:T(8,128)(2,1)S(1)}, u32[]{:S(2)}, u32[]{:S(2)}) collective-permute-start(bf16[2,7,128,128]{3,2,1,0:T(8,128)(2,1)S(1)} %collective-permute-done.1.a_or_p), channel_id=1, source_target_pairs={{0,2},{2,0},{4,6},{6,4},{8,10},{10,8},{12,14},{14,12},{16,18},{18,... | collective-permute-start | bytes 1376264 | tf_op jit(solution)/shard_map/ppermute | solution.py:185

commit v6 on v5

--- a/solution.py
+++ b/solution.py
@@ -12,6 +12,13 @@
 STEPS = 64.0
 F32 = jnp.float32
 BF16 = jnp.bfloat16
+
+
+ORDER = (0, 10)
+
+
+def slot_of(row_index):
+    return row_index ^ jnp.where(lax.axis_index("col") % 2 == 0, ORDER[0], ORDER[1])
 
 
 def code(value):
@@ -49,13 +56,14 @@
             steps, scales = jnp.concatenate(steps, axis=0), jnp.concatenate(scales, axis=0)
             for target in range(out_ref.shape[0]):
                 if out_ref is partner_ref and target == h or out_ref is own_ref and target // 4 % 2 == h:
-                    out_ref[target, 0:BLK, :] = steps.astype(jnp.int16)
-                    out_ref[target, BLK : BLK + SCALE_ROWS, :] = scales.astype(jnp.int16)
+                    slot = target if out_ref is partner_ref else slot_of(target)
+                    out_ref[slot, 0:BLK, :] = steps.astype(jnp.int16)
+                    out_ref[slot, BLK : BLK + SCALE_ROWS, :] = scales.astype(jnp.int16)
 
 
 def spread_kernel(pair_ref, out_ref):
     for target in range(out_ref.shape[0]):
-        out_ref[target] = pair_ref[target // 4 % 2]
+        out_ref[slot_of(target)] = pair_ref[target // 4 % 2]
 
 
 def main_kernel(columns_ref, aggregates_ref, near_ref, far_ref, a_own, p_own, a_or_p, p_or_a, out_ref, total):
@@ -79,7 +87,7 @@
         neighbours = []
         for k in range(slots):
             j = columns_ref[k, i]
-            source = j // 4
+            source = slot_of(j // 4)
             near = (j // 2) % 2 == fiber
             place = pl.ds(pl.multiple_of(j % 2 * HALF, HALF), HALF)
             block, codes = [
@@ -112,16 +120,18 @@
             total[group] += part[:, k * BLK : (k + 1) * BLK]
     for coarse in range(total.shape[0]):
         steps, scale = code(total[coarse])
-        out_ref[coarse, 0:HALF, :] = steps.astype(jnp.int16)
-        out_ref[coarse, HALF : HALF + SCALE_ROWS, :] = jnp.concatenate([scale, scale], axis=0).astype(jnp.int16)
+        slot = slot_of(coarse)
+        out_ref[slot, 0:HALF, :] = steps.astype(jnp.int16)
+        out_ref[slot, HALF : HALF + SCALE_ROWS, :] = jnp.concatenate([scale, scale], axis=0).astype(jnp.int16)
 
 
 def sum_kernel(parts_ref, out_ref):
     halves = [jnp.zeros((HALF, BLK), F32), jnp.zeros((HALF, BLK), F32)]
     for source in range(parts_ref.shape[0]):
         h = (source // 4) % 2
-        factor = scale_of(parts_ref[source, HALF : HALF + SCALE_ROWS, :].astype(jnp.int32))
-        halves[h] = halves[h] + parts_ref[source, 0:HALF, :].astype(jnp.int32).astype(F32) * factor
+        slot = slot_of(source)
+        factor = scale_of(parts_ref[slot, HALF : HALF + SCALE_ROWS, :].astype(jnp.int32))
+        halves[h] = halves[h] + parts_ref[slot, 0:HALF, :].astype(jnp.int32).astype(F32) * factor
     steps, scale = code(jnp.concatenate(halves, axis=0).T)
     out_ref[0:BLK, :] = steps.astype(jnp.int16)
     out_ref[BLK : BLK + SCALE_ROWS, :] = jnp.concatenate([scale, scale], axis=0).astype(jnp.int16)
@@ -156,6 +166,8 @@
     across = [
         (c * nfiber + f, (c + ncol // 2) % ncol * nfiber + 1 - f) for c in range(ncol) for f in range(nfiber)
     ]
+
+    orders = [[(k ^ ORDER[c % 2]) * ncol + c for k in range(nrow)] for c in range(ncol)]
     columns = block_columns.T
     packed_rows = BLK + SCALE_ROWS
     partner, own = pl.pallas_call(
@@ -171,7 +183,7 @@
     here = jnp.where(lax.axis_index("col") % 2 == 0, a_blocks, p_terms)
     from_pair = lax.ppermute(here, "row", pairs)
     crossed = lax.ppermute(partner, ("col", "fiber"), across)
-    near = lax.all_to_all(own, "row", 0, 0, tiled=True)
+    near = lax.all_to_all(own, ("row", "col"), 0, 0, axis_index_groups=orders, tiled=True)
     spread = pl.pallas_call(
         spread_kernel,
         out_shape=jax.ShapeDtypeStruct((nrow, packed_rows, BLK), jnp.int16),
@@ -181,7 +193,7 @@
         compiler_params=pltpu.CompilerParams(vmem_limit_bytes=4 * 1024 * 1024),
         name="spread",
     )(crossed)
-    far = lax.all_to_all(spread, "row", 0, 0, tiled=True)
+    far = lax.all_to_all(spread, ("row", "col"), 0, 0, axis_index_groups=orders, tiled=True)
     from_core = lax.ppermute(from_pair, "col", [(c, c ^ 1) for c in range(ncol)])
     parts = pl.pallas_call(
         main_kernel,
@@ -192,7 +204,7 @@
         compiler_params=pltpu.CompilerParams(vmem_limit_bytes=16 * 1024 * 1024),
         name="main",
     )(columns, aggregates, near, far, a_blocks, p_terms, from_pair, from_core)
-    received = lax.all_to_all(parts, "row", 0, 0, tiled=True)
+    received = lax.all_to_all(parts, ("row", "col"), 0, 0, axis_index_groups=orders, tiled=True)
     tile = pl.pallas_call(
         sum_kernel,
         out_shape=jax.ShapeDtypeStruct((packed_rows, BLK), jnp.int16),

time: 75.1 us -> 74.4 us (level)
  starting transfers between devices: 32.9 us -> 31.1 us
  blocking collectives: 25.3 us -> 26.1 us
    all_to_all x2, starting transfers between devices: 16.7 us -> 14.9 us  [the longest x1 9.34 us: local(): lax.all_to_all(own, ('row', 'col'), 0, 0, axis_index_groups=orders, tiled...]
    all_to_all x2, waiting for transfers between devices: 8.36 us -> 6.99 us  [the longest x1 6.99 us: local(): lax.all_to_all(spread, ('row', 'col'), 0, 0, axis_index_groups=orders, ti...]
    ppermute x1, waiting for transfers between devices: 0.01 us -> 1.25 us  [local(): from_pair = lax.ppermute(here, 'row', pairs)]
    all_to_all x1, blocking collectives: 12 us -> 12.7 us  [local(): lax.all_to_all(parts, ('row', 'col'), 0, 0, axis_index_groups=orders, til...]
  transfers between devices with their start and end apart: 5 -> 5, of which waited for: 2 -> 3; matrix products, arithmetic and copies ran while one was open for 0% -> 0% of each run, Pallas kernels for 1% -> 1%
where the time goes in v6:
time: 74.4 us; the launch traced here: 73.9 us
  starting transfers between devices  31.1 us (42%)
  blocking collectives  26.1 us (35%)
  waiting for transfers between devices  10.9 us (15%)
  Pallas kernels  5.7 us (8%)
    all_gather x1, blocking collectives, local(): layers = lax.all_gather(tile, 'fiber')  13.3 us
    all_to_all x1, blocking collectives, local(): lax.all_to_all(parts, ('row', 'col'), 0, 0, axis_index_groups=orders, til...  12.7 us
    ppermute x1, starting transfers between devices, local(): crossed = lax.ppermute(partner, ('col', 'fiber'), across)  10.9 us
    all_to_all x1, starting transfers between devices, local(): lax.all_to_all(own, ('row', 'col'), 0, 0, axis_index_groups=orders, tiled...  9.34 us
    all_to_all x1, waiting for transfers between devices, local(): lax.all_to_all(spread, ('row', 'col'), 0, 0, axis_index_groups=orders, ti...  6.99 us
    all_to_all x1, starting transfers between devices, local(): lax.all_to_all(spread, ('row', 'col'), 0, 0, axis_index_groups=orders, ti...  5.53 us
    ppermute x1, starting transfers between devices, local(): from_pair = lax.ppermute(here, 'row', pairs)  3.37 us
    ppermute x1, waiting for transfers between devices, local(): crossed = lax.ppermute(partner, ('col', 'fiber'), across)  2.61 us
  transfers between devices with their start and end apart: 5, of which 3 were waited for; matrix products, arithmetic and copies ran while one was open for 0% of the time, Pallas kernels for 1%

profile of v6, /device:TPU:8, one launch (start us, length us, event | category | flops | bytes accessed | tf_op | source)
XLA Modules:
  0.0 73.9 jit_solution(14136007475141917683)
XLA Ops:
  0.0 2.2 %build.1 = (s16[2,144,128]{2,1,0:T(8,128)(2,1)}, s16[16,144,128]{2,1,0:T(8,128)(2,1)}) custom-call(s32[7,64]{1,0:T(8,128)} %bitcast.3, s32[64]{0:T(128)} %aggregates_ref.3, bf16[2,7,128,128]{3,2,1,0:T(8,128)(2,1)} %p_own.1), custom_call_target="tpu_custom_call" | custom-call | tf_op jit(solution)/shard_map/build/pallas_call | solution.py:173
  2.2 0.0 copy-start.4
  2.2 0.0 copy-start
  2.2 0.0 copy-start.1
  2.2 9.3 %all-to-all-start = ((s16[16,144,128]{2,1,0:T(8,128)(2,1)}), s16[16,144,128]{2,1,0:T(8,128)(2,1)S(1)}, u32[]{:S(2)}, u32[]{:S(2)}) async-start(s16[16,144,128]{2,1,0:T(8,128)(2,1)} %get-tuple-element.7), calls=%async_computation | async-start | bytes 1179648 | tf_op jit(solution)/shard_map/all_to_all | solution.py:186
  11.6 0.0 copy-done.4
  11.6 10.9 %collective-permute-start = (s16[2,144,128]{2,1,0:T(8,128)(2,1)S(1)}, s16[2,144,128]{2,1,0:T(8,128)(2,1)S(1)}, u32[]{:S(2)}, u32[]{:S(2)}) collective-permute-start(s16[2,144,128]{2,1,0:T(8,128)(2,1)S(1)} %copy-done.4), channel_id=1, source_target_pairs={{0,17},{1,16},{2,19},{3,18},{4,21},{5,20},{6,23},{7,22},{8,25},{9,... | collective-permute-start | bytes 221192 | tf_op jit(solution)/shard_map/ppermute | solution.py:185
  22.5 0.0 copy-done
  22.5 0.0 copy-done.1
  22.6 0.1 broadcast_select_fusion
  22.6 3.4 %collective-permute-start.1 = (bf16[2,7,128,128]{3,2,1,0:T(8,128)(2,1)S(1)}, bf16[2,7,128,128]{3,2,1,0:T(8,128)(2,1)S(1)}, u32[]{:S(2)}, u32[]{:S(2)}) collective-permute-start(bf16[2,7,128,128]{3,2,1,0:T(8,128)(2,1)S(1)} %broadcast_select_fusion), channel_id=1, source_target_pairs={{0,128},{32,160},{64,192},{96,224},{128,0},{160,32},{192,64},{224,... | collective-permute-start | bytes 1376264 | tf_op jit(solution)/shard_map/ppermute | solution.py:184
  26.0 2.6 %collective-permute-done.pair_ref = s16[2,144,128]{2,1,0:T(8,128)(2,1)S(1)} collective-permute-done((s16[2,144,128]{2,1,0:T(8,128)(2,1)S(1)}, s16[2,144,128]{2,1,0:T(8,128)(2,1)S(1)}, u32[]{:S(2)}, u32[]{:S(2)}) %collective-permute-start) | collective-permute-done | bytes 73760 | tf_op jit(solution)/shard_map/ppermute | solution.py:185
  28.6 0.9 %spread.1 = s16[16,144,128]{2,1,0:T(8,128)(2,1)} custom-call(s16[2,144,128]{2,1,0:T(8,128)(2,1)S(1)} %collective-permute-done.pair_ref), custom_call_target="tpu_custom_call" | custom-call | flops 137438953472 | bytes 2097152 | tf_op jit(solution)/shard_map/spread/pallas_call | solution.py:187
  29.5 0.0 copy-start.2
  29.5 0.0 copy-start.3
  29.5 0.0 all-to-all-done.near_ref
  29.5 5.5 %all-to-all-start.1 = ((s16[16,144,128]{2,1,0:T(8,128)(2,1)}), s16[16,144,128]{2,1,0:T(8,128)(2,1)S(1)}, u32[]{:S(2)}, u32[]{:S(2)}) async-start(s16[16,144,128]{2,1,0:T(8,128)(2,1)} %spread.1), calls=%async_computation.1 | async-start | bytes 1179648 | tf_op jit(solution)/shard_map/all_to_all | solution.py:196
  35.0 1.2 %collective-permute-done.1.a_or_p = bf16[2,7,128,128]{3,2,1,0:T(8,128)(2,1)S(1)} collective-permute-done((bf16[2,7,128,128]{3,2,1,0:T(8,128)(2,1)S(1)}, bf16[2,7,128,128]{3,2,1,0:T(8,128)(2,1)S(1)}, u32[]{:S(2)}, u32[]{:S(2)}) %collective-permute-start.1) | collective-permute-done | bytes 458784 | tf_op jit(solution)/shard_map/ppermute | solution.py:184
  36.3 1.9 %collective-permute-start.2 = (bf16[2,7,128,128]{3,2,1,0:T(8,128)(2,1)S(1)}, bf16[2,7,128,128]{3,2,1,0:T(8,128)(2,1)S(1)}, u32[]{:S(2)}, u32[]{:S(2)}) collective-permute-start(bf16[2,7,128,128]{3,2,1,0:T(8,128)(2,1)S(1)} %collective-permute-done.1.a_or_p), channel_id=1, source_target_pairs={{0,2},{2,0},{4,6},{6,4},{8,10},{10,8},{12,14},{14,12},{16,18},{18,... | collective-permute-start | bytes 1376264 | tf_op jit(solution)/shard_map/ppermute | solution.py:197
  38.2 7.0 %all-to-all-done.1.far_ref = s16[16,144,128]{2,1,0:T(8,128)(2,1)S(1)} async-done(((s16[16,144,128]{2,1,0:T(8,128)(2,1)}), s16[16,144,128]{2,1,0:T(8,128)(2,1)S(1)}, u32[]{:S(2)}, u32[]{:S(2)}) %all-to-all-start.1) | async-done | bytes 589856 | tf_op jit(solution)/shard_map/all_to_all | solution.py:196
  45.2 0.0 collective-permute-done.2.p_or_a
  45.2 0.0 copy-done.2
  45.2 0.0 copy-done.3
  45.2 1.7 %main.1 = s16[16,80,128]{2,1,0:T(8,128)(2,1)S(1)} custom-call(s32[7,64]{1,0:T(8,128)S(1)} %bitcast.4, s32[64]{0:T(128)S(1)} %copy-done.3, s16[16,144,128]{2,1,0:T(8,128)(2,1)S(1)} %all-to-all-done.near_ref, s16[16,144,128]{2,1,0:T(8,128)(2,1)S(1)} %all-to-all-done.1.far_ref, bf16[2,7,128,128]{3,2,1,0:T(8,128)(2,1)S(1)} %copy-done.1, ...), custom_call_target="tpu_custom_call" | custom-call | tf_op jit(solution)/shard_map/main/pallas_call | solution.py:198
  46.9 12.7 %all_to_all.15.parts_ref = s16[16,80,128]{2,1,0:T(8,128)(2,1)S(1)} all-to-all(s16[16,80,128]{2,1,0:T(8,128)(2,1)S(1)} %main.1), channel_id=1, replica_groups={{0,32,64,96,128,160,192,224,256,288,320,352,384,416,448,480},{322,354,2..., dimensions={0} | all-to-all | bytes 655360 | tf_op jit(solution)/shard_map/all_to_all | solution.py:207
  59.7 0.2 sum.1
  59.9 13.3 %all-gather = s16[288,128]{1,0:T(8,128)(2,1)S(1)} all-gather(s16[144,128]{1,0:T(8,128)(2,1)S(1)} %sum.1), channel_id=2, replica_groups=mesh['row'=16,'col'=16,'fiber'=2] {'fiber'}, dimensions={0}, use_global_device_ids=true | all-gather | bytes 110592 | tf_op jit(solution)/shard_map/all_gather | solution.py:216
  73.2 0.6 add.6
Async XLA Ops:
  2.2 9.3 %copy-start.4 = (s16[2,144,128]{2,1,0:T(8,128)(2,1)S(1)}, s16[2,144,128]{2,1,0:T(8,128)(2,1)}, u32[]{:S(2)}) copy-start(s16[2,144,128]{2,1,0:T(8,128)(2,1)} %get-tuple-element.8) | copy-start | bytes 221188
  2.2 20.3 %copy-start = (bf16[2,7,128,128]{3,2,1,0:T(8,128)(2,1)S(1)}, bf16[2,7,128,128]{3,2,1,0:T(8,128)(2,1)}, u32[]{:S(2)}) copy-start(bf16[2,7,128,128]{3,2,1,0:T(8,128)(2,1)} %p_own.1) | copy-start | bytes 1376260
  2.2 20.3 %copy-start.1 = (bf16[2,7,128,128]{3,2,1,0:T(8,128)(2,1)S(1)}, bf16[2,7,128,128]{3,2,1,0:T(8,128)(2,1)}, u32[]{:S(2)}) copy-start(bf16[2,7,128,128]{3,2,1,0:T(8,128)(2,1)} %a_own.1) | copy-start | bytes 1376260
  2.2 27.3 %all-to-all-start = ((s16[16,144,128]{2,1,0:T(8,128)(2,1)}), s16[16,144,128]{2,1,0:T(8,128)(2,1)S(1)}, u32[]{:S(2)}, u32[]{:S(2)}) async-start(s16[16,144,128]{2,1,0:T(8,128)(2,1)} %get-tuple-element.7), calls=%async_computation | async-start | bytes 1179648 | tf_op jit(solution)/shard_map/all_to_all | solution.py:186
  11.6 17.0 %collective-permute-start = (s16[2,144,128]{2,1,0:T(8,128)(2,1)S(1)}, s16[2,144,128]{2,1,0:T(8,128)(2,1)S(1)}, u32[]{:S(2)}, u32[]{:S(2)}) collective-permute-start(s16[2,144,128]{2,1,0:T(8,128)(2,1)S(1)} %copy-done.4), channel_id=1, source_target_pairs={{0,17},{1,16},{2,19},{3,18},{4,21},{5,20},{6,23},{7,22},{8,25},{9,... | collective-permute-start | bytes 221192 | tf_op jit(solution)/shard_map/ppermute | solution.py:185
  22.6 13.7 %collective-permute-start.1 = (bf16[2,7,128,128]{3,2,1,0:T(8,128)(2,1)S(1)}, bf16[2,7,128,128]{3,2,1,0:T(8,128)(2,1)S(1)}, u32[]{:S(2)}, u32[]{:S(2)}) collective-permute-start(bf16[2,7,128,128]{3,2,1,0:T(8,128)(2,1)S(1)} %broadcast_select_fusion), channel_id=1, source_target_pairs={{0,128},{32,160},{64,192},{96,224},{128,0},{160,32},{192,64},{224,... | collective-permute-start | bytes 1376264 | tf_op jit(solution)/shard_map/ppermute | solution.py:184
  29.5 15.7 %copy-start.2 = (s32[64,7]{0,1:T(8,128)S(1)}, s32[64,7]{0,1:T(8,128)}, u32[]{:S(2)}) copy-start(s32[64,7]{0,1:T(8,128)} %param.6) | copy-start | bytes 5380
  29.5 15.7 %copy-start.3 = (s32[64]{0:T(128)S(1)}, s32[64]{0:T(128)}, u32[]{:S(2)}) copy-start(s32[64]{0:T(128)} %aggregates_ref.3) | copy-start | bytes 772
  29.5 15.7 %all-to-all-start.1 = ((s16[16,144,128]{2,1,0:T(8,128)(2,1)}), s16[16,144,128]{2,1,0:T(8,128)(2,1)S(1)}, u32[]{:S(2)}, u32[]{:S(2)}) async-start(s16[16,144,128]{2,1,0:T(8,128)(2,1)} %spread.1), calls=%async_computation.1 | async-start | bytes 1179648 | tf_op jit(solution)/shard_map/all_to_all | solution.py:196
  36.3 8.9 %collective-permute-start.2 = (bf16[2,7,128,128]{3,2,1,0:T(8,128)(2,1)S(1)}, bf16[2,7,128,128]{3,2,1,0:T(8,128)(2,1)S(1)}, u32[]{:S(2)}, u32[]{:S(2)}) collective-permute-start(bf16[2,7,128,128]{3,2,1,0:T(8,128)(2,1)S(1)} %collective-permute-done.1.a_or_p), channel_id=1, source_target_pairs={{0,2},{2,0},{4,6},{6,4},{8,10},{10,8},{12,14},{14,12},{16,18},{18,... | collective-permute-start | bytes 1376264 | tf_op jit(solution)/shard_map/ppermute | solution.py:197

commit v7 on v6

--- a/solution.py
+++ b/solution.py
@@ -14,11 +14,12 @@
 BF16 = jnp.bfloat16
 
 
-ORDER = (0, 10)
-
-
-def slot_of(row_index):
-    return row_index ^ jnp.where(lax.axis_index("col") % 2 == 0, ORDER[0], ORDER[1])
+NEAR = (0, 10)
+LATER = (10, 5)
+
+
+def slot_of(row_index, masks):
+    return row_index ^ jnp.where(lax.axis_index("col") % 2 == 0, masks[0], masks[1])
 
 
 def code(value):
@@ -56,14 +57,14 @@
             steps, scales = jnp.concatenate(steps, axis=0), jnp.concatenate(scales, axis=0)
             for target in range(out_ref.shape[0]):
                 if out_ref is partner_ref and target == h or out_ref is own_ref and target // 4 % 2 == h:
-                    slot = target if out_ref is partner_ref else slot_of(target)
+                    slot = target if out_ref is partner_ref else slot_of(target, NEAR)
                     out_ref[slot, 0:BLK, :] = steps.astype(jnp.int16)
                     out_ref[slot, BLK : BLK + SCALE_ROWS, :] = scales.astype(jnp.int16)
 
 
 def spread_kernel(pair_ref, out_ref):
     for target in range(out_ref.shape[0]):
-        out_ref[slot_of(target)] = pair_ref[target // 4 % 2]
+        out_ref[slot_of(target, LATER)] = pair_ref[target // 4 % 2]
 
 
 def main_kernel(columns_ref, aggregates_ref, near_ref, far_ref, a_own, p_own, a_or_p, p_or_a, out_ref, total):
@@ -87,11 +88,11 @@
         neighbours = []
         for k in range(slots):
             j = columns_ref[k, i]
-            source = slot_of(j // 4)
+            near_slot, far_slot = slot_of(j // 4, NEAR), slot_of(j // 4, LATER)
             near = (j // 2) % 2 == fiber
             place = pl.ds(pl.multiple_of(j % 2 * HALF, HALF), HALF)
             block, codes = [
-                jnp.where(near, near_ref[source, part].astype(jnp.int32), far_ref[source, part].astype(jnp.int32))
+                jnp.where(near, near_ref[near_slot, part].astype(jnp.int32), far_ref[far_slot, part].astype(jnp.int32))
                 for part in (place, slice(BLK, BLK + SCALE_ROWS))
             ]
             codes = jnp.where(j % 2 == 0, codes[0:1], codes[SCALE_ROWS // 2 : SCALE_ROWS // 2 + 1])
@@ -120,7 +121,7 @@
             total[group] += part[:, k * BLK : (k + 1) * BLK]
     for coarse in range(total.shape[0]):
         steps, scale = code(total[coarse])
-        slot = slot_of(coarse)
+        slot = slot_of(coarse, LATER)
         out_ref[slot, 0:HALF, :] = steps.astype(jnp.int16)
         out_ref[slot, HALF : HALF + SCALE_ROWS, :] = jnp.concatenate([scale, scale], axis=0).astype(jnp.int16)
 
@@ -129,7 +130,7 @@
     halves = [jnp.zeros((HALF, BLK), F32), jnp.zeros((HALF, BLK), F32)]
     for source in range(parts_ref.shape[0]):
         h = (source // 4) % 2
-        slot = slot_of(source)
+        slot = slot_of(source, LATER)
         factor = scale_of(parts_ref[slot, HALF : HALF + SCALE_ROWS, :].astype(jnp.int32))
         halves[h] = halves[h] + parts_ref[slot, 0:HALF, :].astype(jnp.int32).astype(F32) * factor
     steps, scale = code(jnp.concatenate(halves, axis=0).T)
@@ -167,7 +168,9 @@
         (c * nfiber + f, (c + ncol // 2) % ncol * nfiber + 1 - f) for c in range(ncol) for f in range(nfiber)
     ]
 
-    orders = [[(k ^ ORDER[c % 2]) * ncol + c for k in range(nrow)] for c in range(ncol)]
+    def orders(masks):
+        return [[(k ^ masks[c % 2]) * ncol + c for k in range(nrow)] for c in range(ncol)]
+
     columns = block_columns.T
     packed_rows = BLK + SCALE_ROWS
     partner, own = pl.pallas_call(
@@ -183,7 +186,7 @@
     here = jnp.where(lax.axis_index("col") % 2 == 0, a_blocks, p_terms)
     from_pair = lax.ppermute(here, "row", pairs)
     crossed = lax.ppermute(partner, ("col", "fiber"), across)
-    near = lax.all_to_all(own, ("row", "col"), 0, 0, axis_index_groups=orders, tiled=True)
+    near = lax.all_to_all(own, ("row", "col"), 0, 0, axis_index_groups=orders(NEAR), tiled=True)
     spread = pl.pallas_call(
         spread_kernel,
         out_shape=jax.ShapeDtypeStruct((nrow, packed_rows, BLK), jnp.int16),
@@ -193,7 +196,7 @@
         compiler_params=pltpu.CompilerParams(vmem_limit_bytes=4 * 1024 * 1024),
         name="spread",
     )(crossed)
-    far = lax.all_to_all(spread, ("row", "col"), 0, 0, axis_index_groups=orders, tiled=True)
+    far = lax.all_to_all(spread, ("row", "col"), 0, 0, axis_index_groups=orders(LATER), tiled=True)
     from_core = lax.ppermute(from_pair, "col", [(c, c ^ 1) for c in range(ncol)])
     parts = pl.pallas_call(
         main_kernel,
@@ -204,7 +207,7 @@
         compiler_params=pltpu.CompilerParams(vmem_limit_bytes=16 * 1024 * 1024),
         name="main",
     )(columns, aggregates, near, far, a_blocks, p_terms, from_pair, from_core)
-    received = lax.all_to_all(parts, ("row", "col"), 0, 0, axis_index_groups=orders, tiled=True)
+    received = lax.all_to_all(parts, ("row", "col"), 0, 0, axis_index_groups=orders(LATER), tiled=True)
     tile = pl.pallas_call(
         sum_kernel,
         out_shape=jax.ShapeDtypeStruct((packed_rows, BLK), jnp.int16),

time: 74.4 us -> 73.4 us (0.987)
  the two profiles are of different devices: /device:TPU:8 before, /device:TPU:2 now
where the time goes in v7:
time: 73.4 us; the launch traced here: 73 us
  starting transfers between devices  30.3 us (41%)
  blocking collectives  26.6 us (36%)
  waiting for transfers between devices  10.2 us (14%)
  Pallas kernels  5.71 us (8%)
    all_gather x1, blocking collectives, local(): layers = lax.all_gather(tile, 'fiber')  13.3 us
    all_to_all x1, blocking collectives, local(): lax.all_to_all(parts, ('row', 'col'), 0, 0, axis_index_groups=orders(LATE...  13.2 us
    ppermute x1, starting transfers between devices, local(): crossed = lax.ppermute(partner, ('col', 'fiber'), across)  10.9 us
    all_to_all x1, starting transfers between devices, local(): lax.all_to_all(own, ('row', 'col'), 0, 0, axis_index_groups=orders(NEAR),...  9.44 us
    all_to_all x1, starting transfers between devices, local(): lax.all_to_all(spread, ('row', 'col'), 0, 0, axis_index_groups=orders(LAT...  6.03 us
    all_to_all x1, waiting for transfers between devices, local(): lax.all_to_all(spread, ('row', 'col'), 0, 0, axis_index_groups=orders(LAT...  4.46 us
    ppermute x1, waiting for transfers between devices, local(): crossed = lax.ppermute(partner, ('col', 'fiber'), across)  3.99 us
    pallas_call x1, Pallas kernels, local(): pl.pallas_call(build_kernel, out_shape=(jax.ShapeDtypeStruct((2, packed_r...  2.23 us
  transfers between devices with their start and end apart: 5, of which 3 were waited for; matrix products, arithmetic and copies ran while one was open for 0% of the time, Pallas kernels for 1%

profile of v7, /device:TPU:2, one launch (start us, length us, event | category | flops | bytes accessed | tf_op | source)
XLA Modules:
  0.0 73.0 jit_solution(7321567996029691940)
XLA Ops:
  0.0 2.2 %build.1 = (s16[2,144,128]{2,1,0:T(8,128)(2,1)}, s16[16,144,128]{2,1,0:T(8,128)(2,1)}) custom-call(s32[7,64]{1,0:T(8,128)} %bitcast.3, s32[64]{0:T(128)} %aggregates_ref.3, bf16[2,7,128,128]{3,2,1,0:T(8,128)(2,1)} %p_own.1), custom_call_target="tpu_custom_call" | custom-call | tf_op jit(solution)/shard_map/build/pallas_call | solution.py:176
  2.2 0.0 copy-start.4
  2.2 0.0 copy-start
  2.2 0.0 copy-start.1
  2.2 9.4 %all-to-all-start = ((s16[16,144,128]{2,1,0:T(8,128)(2,1)}), s16[16,144,128]{2,1,0:T(8,128)(2,1)S(1)}, u32[]{:S(2)}, u32[]{:S(2)}) async-start(s16[16,144,128]{2,1,0:T(8,128)(2,1)} %get-tuple-element.7), calls=%async_computation | async-start | bytes 1179648 | tf_op jit(solution)/shard_map/all_to_all | solution.py:189
  11.7 0.0 copy-done.4
  11.7 10.9 %collective-permute-start = (s16[2,144,128]{2,1,0:T(8,128)(2,1)S(1)}, s16[2,144,128]{2,1,0:T(8,128)(2,1)S(1)}, u32[]{:S(2)}, u32[]{:S(2)}) collective-permute-start(s16[2,144,128]{2,1,0:T(8,128)(2,1)S(1)} %copy-done.4), channel_id=1, source_target_pairs={{0,17},{1,16},{2,19},{3,18},{4,21},{5,20},{6,23},{7,22},{8,25},{9,... | collective-permute-start | bytes 221192 | tf_op jit(solution)/shard_map/ppermute | solution.py:188
  22.6 0.0 copy-done
  22.6 0.0 copy-done.1
  22.6 0.1 broadcast_select_fusion
  22.7 2.0 %collective-permute-start.1 = (bf16[2,7,128,128]{3,2,1,0:T(8,128)(2,1)S(1)}, bf16[2,7,128,128]{3,2,1,0:T(8,128)(2,1)S(1)}, u32[]{:S(2)}, u32[]{:S(2)}) collective-permute-start(bf16[2,7,128,128]{3,2,1,0:T(8,128)(2,1)S(1)} %broadcast_select_fusion), channel_id=1, source_target_pairs={{0,128},{32,160},{64,192},{96,224},{128,0},{160,32},{192,64},{224,... | collective-permute-start | bytes 1376264 | tf_op jit(solution)/shard_map/ppermute | solution.py:187
  24.7 4.0 %collective-permute-done.pair_ref = s16[2,144,128]{2,1,0:T(8,128)(2,1)S(1)} collective-permute-done((s16[2,144,128]{2,1,0:T(8,128)(2,1)S(1)}, s16[2,144,128]{2,1,0:T(8,128)(2,1)S(1)}, u32[]{:S(2)}, u32[]{:S(2)}) %collective-permute-start) | collective-permute-done | bytes 73760 | tf_op jit(solution)/shard_map/ppermute | solution.py:188
  28.7 0.9 %spread.1 = s16[16,144,128]{2,1,0:T(8,128)(2,1)} custom-call(s16[2,144,128]{2,1,0:T(8,128)(2,1)S(1)} %collective-permute-done.pair_ref), custom_call_target="tpu_custom_call" | custom-call | flops 137438953472 | bytes 2097152 | tf_op jit(solution)/shard_map/spread/pallas_call | solution.py:190
  29.6 0.0 copy-start.2
  29.6 0.0 copy-start.3
  29.6 0.0 all-to-all-done.near_ref
  29.6 6.0 %all-to-all-start.1 = ((s16[16,144,128]{2,1,0:T(8,128)(2,1)}), s16[16,144,128]{2,1,0:T(8,128)(2,1)S(1)}, u32[]{:S(2)}, u32[]{:S(2)}) async-start(s16[16,144,128]{2,1,0:T(8,128)(2,1)} %spread.1), calls=%async_computation.1 | async-start | bytes 1179648 | tf_op jit(solution)/shard_map/all_to_all | solution.py:199
  35.6 1.7 %collective-permute-done.1.a_or_p = bf16[2,7,128,128]{3,2,1,0:T(8,128)(2,1)S(1)} collective-permute-done((bf16[2,7,128,128]{3,2,1,0:T(8,128)(2,1)S(1)}, bf16[2,7,128,128]{3,2,1,0:T(8,128)(2,1)S(1)}, u32[]{:S(2)}, u32[]{:S(2)}) %collective-permute-start.1) | collective-permute-done | bytes 458784 | tf_op jit(solution)/shard_map/ppermute | solution.py:187
  37.4 1.9 %collective-permute-start.2 = (bf16[2,7,128,128]{3,2,1,0:T(8,128)(2,1)S(1)}, bf16[2,7,128,128]{3,2,1,0:T(8,128)(2,1)S(1)}, u32[]{:S(2)}, u32[]{:S(2)}) collective-permute-start(bf16[2,7,128,128]{3,2,1,0:T(8,128)(2,1)S(1)} %collective-permute-done.1.a_or_p), channel_id=1, source_target_pairs={{0,2},{2,0},{4,6},{6,4},{8,10},{10,8},{12,14},{14,12},{16,18},{18,... | collective-permute-start | bytes 1376264 | tf_op jit(solution)/shard_map/ppermute | solution.py:200
  39.3 4.5 %all-to-all-done.1.far_ref = s16[16,144,128]{2,1,0:T(8,128)(2,1)S(1)} async-done(((s16[16,144,128]{2,1,0:T(8,128)(2,1)}), s16[16,144,128]{2,1,0:T(8,128)(2,1)S(1)}, u32[]{:S(2)}, u32[]{:S(2)}) %all-to-all-start.1) | async-done | bytes 589856 | tf_op jit(solution)/shard_map/all_to_all | solution.py:199
  43.8 0.0 collective-permute-done.2.p_or_a
  43.8 0.0 copy-done.2
  43.8 0.0 copy-done.3
  43.8 1.7 %main.1 = s16[16,80,128]{2,1,0:T(8,128)(2,1)S(1)} custom-call(s32[7,64]{1,0:T(8,128)S(1)} %bitcast.4, s32[64]{0:T(128)S(1)} %copy-done.3, s16[16,144,128]{2,1,0:T(8,128)(2,1)S(1)} %all-to-all-done.near_ref, s16[16,144,128]{2,1,0:T(8,128)(2,1)S(1)} %all-to-all-done.1.far_ref, bf16[2,7,128,128]{3,2,1,0:T(8,128)(2,1)S(1)} %copy-done.1, ...), custom_call_target="tpu_custom_call" | custom-call | tf_op jit(solution)/shard_map/main/pallas_call | solution.py:201
  45.5 13.2 %all_to_all.15.parts_ref = s16[16,80,128]{2,1,0:T(8,128)(2,1)S(1)} all-to-all(s16[16,80,128]{2,1,0:T(8,128)(2,1)S(1)} %main.1), channel_id=1, replica_groups={{320,352,256,288,448,480,384,416,64,96,0,32,192,224,128,160},{162,130,2..., dimensions={0} | all-to-all | bytes 655360 | tf_op jit(solution)/shard_map/all_to_all | solution.py:210
  58.8 0.2 sum.1
  59.0 13.3 %all-gather = s16[288,128]{1,0:T(8,128)(2,1)S(1)} all-gather(s16[144,128]{1,0:T(8,128)(2,1)S(1)} %sum.1), channel_id=2, replica_groups=mesh['row'=16,'col'=16,'fiber'=2] {'fiber'}, dimensions={0}, use_global_device_ids=true | all-gather | bytes 110592 | tf_op jit(solution)/shard_map/all_gather | solution.py:219
  72.3 0.6 add.6
Async XLA Ops:
  2.2 9.5 %copy-start.4 = (s16[2,144,128]{2,1,0:T(8,128)(2,1)S(1)}, s16[2,144,128]{2,1,0:T(8,128)(2,1)}, u32[]{:S(2)}) copy-start(s16[2,144,128]{2,1,0:T(8,128)(2,1)} %get-tuple-element.8) | copy-start | bytes 221188
  2.2 20.4 %copy-start = (bf16[2,7,128,128]{3,2,1,0:T(8,128)(2,1)S(1)}, bf16[2,7,128,128]{3,2,1,0:T(8,128)(2,1)}, u32[]{:S(2)}) copy-start(bf16[2,7,128,128]{3,2,1,0:T(8,128)(2,1)} %p_own.1) | copy-start | bytes 1376260
  2.2 20.4 %copy-start.1 = (bf16[2,7,128,128]{3,2,1,0:T(8,128)(2,1)S(1)}, bf16[2,7,128,128]{3,2,1,0:T(8,128)(2,1)}, u32[]{:S(2)}) copy-start(bf16[2,7,128,128]{3,2,1,0:T(8,128)(2,1)} %a_own.1) | copy-start | bytes 1376260
  2.2 27.4 %all-to-all-start = ((s16[16,144,128]{2,1,0:T(8,128)(2,1)}), s16[16,144,128]{2,1,0:T(8,128)(2,1)S(1)}, u32[]{:S(2)}, u32[]{:S(2)}) async-start(s16[16,144,128]{2,1,0:T(8,128)(2,1)} %get-tuple-element.7), calls=%async_computation | async-start | bytes 1179648 | tf_op jit(solution)/shard_map/all_to_all | solution.py:189
  11.7 17.0 %collective-permute-start = (s16[2,144,128]{2,1,0:T(8,128)(2,1)S(1)}, s16[2,144,128]{2,1,0:T(8,128)(2,1)S(1)}, u32[]{:S(2)}, u32[]{:S(2)}) collective-permute-start(s16[2,144,128]{2,1,0:T(8,128)(2,1)S(1)} %copy-done.4), channel_id=1, source_target_pairs={{0,17},{1,16},{2,19},{3,18},{4,21},{5,20},{6,23},{7,22},{8,25},{9,... | collective-permute-start | bytes 221192 | tf_op jit(solution)/shard_map/ppermute | solution.py:188
  22.7 14.7 %collective-permute-start.1 = (bf16[2,7,128,128]{3,2,1,0:T(8,128)(2,1)S(1)}, bf16[2,7,128,128]{3,2,1,0:T(8,128)(2,1)S(1)}, u32[]{:S(2)}, u32[]{:S(2)}) collective-permute-start(bf16[2,7,128,128]{3,2,1,0:T(8,128)(2,1)S(1)} %broadcast_select_fusion), channel_id=1, source_target_pairs={{0,128},{32,160},{64,192},{96,224},{128,0},{160,32},{192,64},{224,... | collective-permute-start | bytes 1376264 | tf_op jit(solution)/shard_map/ppermute | solution.py:187
  29.6 14.2 %copy-start.2 = (s32[64,7]{0,1:T(8,128)S(1)}, s32[64,7]{0,1:T(8,128)}, u32[]{:S(2)}) copy-start(s32[64,7]{0,1:T(8,128)} %param.6) | copy-start | bytes 5380
  29.6 14.2 %copy-start.3 = (s32[64]{0:T(128)S(1)}, s32[64]{0:T(128)}, u32[]{:S(2)}) copy-start(s32[64]{0:T(128)} %aggregates_ref.3) | copy-start | bytes 772
  29.6 14.1 %all-to-all-start.1 = ((s16[16,144,128]{2,1,0:T(8,128)(2,1)}), s16[16,144,128]{2,1,0:T(8,128)(2,1)S(1)}, u32[]{:S(2)}, u32[]{:S(2)}) async-start(s16[16,144,128]{2,1,0:T(8,128)(2,1)} %spread.1), calls=%async_computation.1 | async-start | bytes 1179648 | tf_op jit(solution)/shard_map/all_to_all | solution.py:199
  37.4 6.4 %collective-permute-start.2 = (bf16[2,7,128,128]{3,2,1,0:T(8,128)(2,1)S(1)}, bf16[2,7,128,128]{3,2,1,0:T(8,128)(2,1)S(1)}, u32[]{:S(2)}, u32[]{:S(2)}) collective-permute-start(bf16[2,7,128,128]{3,2,1,0:T(8,128)(2,1)S(1)} %collective-permute-done.1.a_or_p), channel_id=1, source_target_pairs={{0,2},{2,0},{4,6},{6,4},{8,10},{10,8},{12,14},{14,12},{16,18},{18,... | collective-permute-start | bytes 1376264 | tf_op jit(solution)/shard_map/ppermute | solution.py:200

commit v8 on v7

--- a/solution.py
+++ b/solution.py
@@ -16,6 +16,14 @@
 
 NEAR = (0, 10)
 LATER = (10, 5)
+
+
+def turned(row_index):
+    return row_index % 4 * 4 + row_index // 4
+
+
+def later_slot(row_index):
+    return jnp.where(lax.axis_index("col") % 2 == 0, turned(row_index ^ LATER[0]), turned(row_index ^ LATER[1]))
 
 
 def slot_of(row_index, masks):
@@ -64,7 +72,7 @@
 
 def spread_kernel(pair_ref, out_ref):
     for target in range(out_ref.shape[0]):
-        out_ref[slot_of(target, LATER)] = pair_ref[target // 4 % 2]
+        out_ref[later_slot(target)] = pair_ref[target // 4 % 2]
 
 
 def main_kernel(columns_ref, aggregates_ref, near_ref, far_ref, a_own, p_own, a_or_p, p_or_a, out_ref, total):
@@ -88,7 +96,7 @@
         neighbours = []
         for k in range(slots):
             j = columns_ref[k, i]
-            near_slot, far_slot = slot_of(j // 4, NEAR), slot_of(j // 4, LATER)
+            near_slot, far_slot = slot_of(j // 4, NEAR), later_slot(j // 4)
             near = (j // 2) % 2 == fiber
             place = pl.ds(pl.multiple_of(j % 2 * HALF, HALF), HALF)
             block, codes = [
@@ -121,7 +129,7 @@
             total[group] += part[:, k * BLK : (k + 1) * BLK]
     for coarse in range(total.shape[0]):
         steps, scale = code(total[coarse])
-        slot = slot_of(coarse, LATER)
+        slot = later_slot(coarse)
         out_ref[slot, 0:HALF, :] = steps.astype(jnp.int16)
         out_ref[slot, HALF : HALF + SCALE_ROWS, :] = jnp.concatenate([scale, scale], axis=0).astype(jnp.int16)
 
@@ -130,7 +138,7 @@
     halves = [jnp.zeros((HALF, BLK), F32), jnp.zeros((HALF, BLK), F32)]
     for source in range(parts_ref.shape[0]):
         h = (source // 4) % 2
-        slot = slot_of(source, LATER)
+        slot = later_slot(source)
         factor = scale_of(parts_ref[slot, HALF : HALF + SCALE_ROWS, :].astype(jnp.int32))
         halves[h] = halves[h] + parts_ref[slot, 0:HALF, :].astype(jnp.int32).astype(F32) * factor
     steps, scale = code(jnp.concatenate(halves, axis=0).T)
@@ -167,6 +175,8 @@
     across = [
         (c * nfiber + f, (c + ncol // 2) % ncol * nfiber + 1 - f) for c in range(ncol) for f in range(nfiber)
     ]
+
+    later = [[(turned(k) ^ LATER[c % 2]) * ncol + c for k in range(nrow)] for c in range(ncol)]
 
     def orders(masks):
         return [[(k ^ masks[c % 2]) * ncol + c for k in range(nrow)] for c in range(ncol)]
@@ -196,7 +206,7 @@
         compiler_params=pltpu.CompilerParams(vmem_limit_bytes=4 * 1024 * 1024),
         name="spread",
     )(crossed)
-    far = lax.all_to_all(spread, ("row", "col"), 0, 0, axis_index_groups=orders(LATER), tiled=True)
+    far = lax.all_to_all(spread, ("row", "col"), 0, 0, axis_index_groups=later, tiled=True)
     from_core = lax.ppermute(from_pair, "col", [(c, c ^ 1) for c in range(ncol)])
     parts = pl.pallas_call(
         main_kernel,
@@ -207,7 +217,7 @@
         compiler_params=pltpu.CompilerParams(vmem_limit_bytes=16 * 1024 * 1024),
         name="main",
     )(columns, aggregates, near, far, a_blocks, p_terms, from_pair, from_core)
-    received = lax.all_to_all(parts, ("row", "col"), 0, 0, axis_index_groups=orders(LATER), tiled=True)
+    received = lax.all_to_all(parts, ("row", "col"), 0, 0, axis_index_groups=later, tiled=True)
     tile = pl.pallas_call(
         sum_kernel,
         out_shape=jax.ShapeDtypeStruct((packed_rows, BLK), jnp.int16),

time: 73.4 us -> 73 us (level)
  the two profiles are of different devices: /device:TPU:2 before, /device:TPU:1 now
where the time goes in v8:
time: 73 us; the launch traced here: 72.6 us
  starting transfers between devices  30.2 us (41%)
  blocking collectives  24.3 us (33%)
  waiting for transfers between devices  11.9 us (16%)
  Pallas kernels  6 us (8%)
    ppermute x1, starting transfers between devices, local(): crossed = lax.ppermute(partner, ('col', 'fiber'), across)  12.5 us
    all_gather x1, blocking collectives, local(): layers = lax.all_gather(tile, 'fiber')  12.3 us
    all_to_all x1, blocking collectives, local(): lax.all_to_all(parts, ('row', 'col'), 0, 0, axis_index_groups=later, tile...  12 us
    all_to_all x1, starting transfers between devices, local(): lax.all_to_all(own, ('row', 'col'), 0, 0, axis_index_groups=orders(NEAR),...  9.78 us
    all_to_all x1, waiting for transfers between devices, local(): lax.all_to_all(spread, ('row', 'col'), 0, 0, axis_index_groups=later, til...  4.75 us
    ppermute x1, waiting for transfers between devices, local(): crossed = lax.ppermute(partner, ('col', 'fiber'), across)  4.16 us
    all_to_all x1, starting transfers between devices, local(): lax.all_to_all(spread, ('row', 'col'), 0, 0, axis_index_groups=later, til...  3.79 us
    ppermute x1, waiting for transfers between devices, local(): from_pair = lax.ppermute(here, 'row', pairs)  3.01 us
  transfers between devices with their start and end apart: 5, of which 3 were waited for; matrix products, arithmetic and copies ran while one was open for 0% of the time, Pallas kernels for 1%

profile of v8, /device:TPU:1, one launch (start us, length us, event | category | flops | bytes accessed | tf_op | source)
XLA Modules:
  0.0 72.6 jit_solution(6414134403071105599)
XLA Ops:
  0.0 2.2 %build.1 = (s16[2,144,128]{2,1,0:T(8,128)(2,1)}, s16[16,144,128]{2,1,0:T(8,128)(2,1)}) custom-call(s32[7,64]{1,0:T(8,128)} %bitcast.3, s32[64]{0:T(128)} %aggregates_ref.3, bf16[2,7,128,128]{3,2,1,0:T(8,128)(2,1)} %p_own.1), custom_call_target="tpu_custom_call" | custom-call | tf_op jit(solution)/shard_map/build/pallas_call | solution.py:186
  2.2 0.0 copy-start.4
  2.2 0.0 copy-start
  2.2 0.0 copy-start.1
  2.2 9.8 %all-to-all-start = ((s16[16,144,128]{2,1,0:T(8,128)(2,1)}), s16[16,144,128]{2,1,0:T(8,128)(2,1)S(1)}, u32[]{:S(2)}, u32[]{:S(2)}) async-start(s16[16,144,128]{2,1,0:T(8,128)(2,1)} %get-tuple-element.7), calls=%async_computation | async-start | bytes 1179648 | tf_op jit(solution)/shard_map/all_to_all | solution.py:199
  12.0 0.0 copy-done.4
  12.0 12.5 %collective-permute-start = (s16[2,144,128]{2,1,0:T(8,128)(2,1)S(1)}, s16[2,144,128]{2,1,0:T(8,128)(2,1)S(1)}, u32[]{:S(2)}, u32[]{:S(2)}) collective-permute-start(s16[2,144,128]{2,1,0:T(8,128)(2,1)S(1)} %copy-done.4), channel_id=1, source_target_pairs={{0,17},{1,16},{2,19},{3,18},{4,21},{5,20},{6,23},{7,22},{8,25},{9,... | collective-permute-start | bytes 221192 | tf_op jit(solution)/shard_map/ppermute | solution.py:198
  24.5 0.0 copy-done
  24.5 0.0 copy-done.1
  24.5 0.1 broadcast_select_fusion
  24.6 1.9 %collective-permute-start.1 = (bf16[2,7,128,128]{3,2,1,0:T(8,128)(2,1)S(1)}, bf16[2,7,128,128]{3,2,1,0:T(8,128)(2,1)S(1)}, u32[]{:S(2)}, u32[]{:S(2)}) collective-permute-start(bf16[2,7,128,128]{3,2,1,0:T(8,128)(2,1)S(1)} %broadcast_select_fusion), channel_id=1, source_target_pairs={{0,128},{32,160},{64,192},{96,224},{128,0},{160,32},{192,64},{224,... | collective-permute-start | bytes 1376264 | tf_op jit(solution)/shard_map/ppermute | solution.py:197
  26.5 4.2 %collective-permute-done.pair_ref = s16[2,144,128]{2,1,0:T(8,128)(2,1)S(1)} collective-permute-done((s16[2,144,128]{2,1,0:T(8,128)(2,1)S(1)}, s16[2,144,128]{2,1,0:T(8,128)(2,1)S(1)}, u32[]{:S(2)}, u32[]{:S(2)}) %collective-permute-start) | collective-permute-done | bytes 73760 | tf_op jit(solution)/shard_map/ppermute | solution.py:198
  30.7 0.9 %spread.1 = s16[16,144,128]{2,1,0:T(8,128)(2,1)} custom-call(s16[2,144,128]{2,1,0:T(8,128)(2,1)S(1)} %collective-permute-done.pair_ref), custom_call_target="tpu_custom_call" | custom-call | flops 137438953472 | bytes 2097152 | tf_op jit(solution)/shard_map/spread/pallas_call | solution.py:200
  31.6 0.0 copy-start.2
  31.6 0.0 copy-start.3
  31.6 0.0 all-to-all-done.near_ref
  31.6 3.8 %all-to-all-start.1 = ((s16[16,144,128]{2,1,0:T(8,128)(2,1)}), s16[16,144,128]{2,1,0:T(8,128)(2,1)S(1)}, u32[]{:S(2)}, u32[]{:S(2)}) async-start(s16[16,144,128]{2,1,0:T(8,128)(2,1)} %spread.1), calls=%async_computation.1 | async-start | bytes 1179648 | tf_op jit(solution)/shard_map/all_to_all | solution.py:209
  35.4 3.0 %collective-permute-done.1.a_or_p = bf16[2,7,128,128]{3,2,1,0:T(8,128)(2,1)S(1)} collective-permute-done((bf16[2,7,128,128]{3,2,1,0:T(8,128)(2,1)S(1)}, bf16[2,7,128,128]{3,2,1,0:T(8,128)(2,1)S(1)}, u32[]{:S(2)}, u32[]{:S(2)}) %collective-permute-start.1) | collective-permute-done | bytes 458784 | tf_op jit(solution)/shard_map/ppermute | solution.py:197
  38.4 2.2 %collective-permute-start.2 = (bf16[2,7,128,128]{3,2,1,0:T(8,128)(2,1)S(1)}, bf16[2,7,128,128]{3,2,1,0:T(8,128)(2,1)S(1)}, u32[]{:S(2)}, u32[]{:S(2)}) collective-permute-start(bf16[2,7,128,128]{3,2,1,0:T(8,128)(2,1)S(1)} %collective-permute-done.1.a_or_p), channel_id=1, source_target_pairs={{0,2},{2,0},{4,6},{6,4},{8,10},{10,8},{12,14},{14,12},{16,18},{18,... | collective-permute-start | bytes 1376264 | tf_op jit(solution)/shard_map/ppermute | solution.py:210
  40.6 4.8 %all-to-all-done.1.far_ref = s16[16,144,128]{2,1,0:T(8,128)(2,1)S(1)} async-done(((s16[16,144,128]{2,1,0:T(8,128)(2,1)}), s16[16,144,128]{2,1,0:T(8,128)(2,1)S(1)}, u32[]{:S(2)}, u32[]{:S(2)}) %all-to-all-start.1) | async-done | bytes 589856 | tf_op jit(solution)/shard_map/all_to_all | solution.py:209
  45.4 0.0 collective-permute-done.2.p_or_a
  45.4 0.0 copy-done.2
  45.4 0.0 copy-done.3
  45.4 2.0 %main.1 = s16[16,80,128]{2,1,0:T(8,128)(2,1)S(1)} custom-call(s32[7,64]{1,0:T(8,128)S(1)} %bitcast.4, s32[64]{0:T(128)S(1)} %copy-done.3, s16[16,144,128]{2,1,0:T(8,128)(2,1)S(1)} %all-to-all-done.near_ref, s16[16,144,128]{2,1,0:T(8,128)(2,1)S(1)} %all-to-all-done.1.far_ref, bf16[2,7,128,128]{3,2,1,0:T(8,128)(2,1)S(1)} %copy-done.1, ...), custom_call_target="tpu_custom_call" | custom-call | tf_op jit(solution)/shard_map/main/pallas_call | solution.py:211
  47.4 12.0 %all_to_all.15.parts_ref = s16[16,80,128]{2,1,0:T(8,128)(2,1)S(1)} all-to-all(s16[16,80,128]{2,1,0:T(8,128)(2,1)S(1)} %main.1), channel_id=1, replica_groups={{320,448,64,192,352,480,96,224,256,384,0,128,288,416,32,160},{162,34,41..., dimensions={0} | all-to-all | bytes 655360 | tf_op jit(solution)/shard_map/all_to_all | solution.py:220
  59.4 0.2 sum.1
  59.6 12.3 %all-gather = s16[288,128]{1,0:T(8,128)(2,1)S(1)} all-gather(s16[144,128]{1,0:T(8,128)(2,1)S(1)} %sum.1), channel_id=2, replica_groups=mesh['row'=16,'col'=16,'fiber'=2] {'fiber'}, dimensions={0}, use_global_device_ids=true | all-gather | bytes 110592 | tf_op jit(solution)/shard_map/all_gather | solution.py:229
  71.9 0.6 add.6
Async XLA Ops:
  2.2 9.8 %copy-start.4 = (s16[2,144,128]{2,1,0:T(8,128)(2,1)S(1)}, s16[2,144,128]{2,1,0:T(8,128)(2,1)}, u32[]{:S(2)}) copy-start(s16[2,144,128]{2,1,0:T(8,128)(2,1)} %get-tuple-element.8) | copy-start | bytes 221188
  2.2 22.3 %copy-start = (bf16[2,7,128,128]{3,2,1,0:T(8,128)(2,1)S(1)}, bf16[2,7,128,128]{3,2,1,0:T(8,128)(2,1)}, u32[]{:S(2)}) copy-start(bf16[2,7,128,128]{3,2,1,0:T(8,128)(2,1)} %p_own.1) | copy-start | bytes 1376260
  2.2 22.3 %copy-start.1 = (bf16[2,7,128,128]{3,2,1,0:T(8,128)(2,1)S(1)}, bf16[2,7,128,128]{3,2,1,0:T(8,128)(2,1)}, u32[]{:S(2)}) copy-start(bf16[2,7,128,128]{3,2,1,0:T(8,128)(2,1)} %a_own.1) | copy-start | bytes 1376260
  2.2 29.3 %all-to-all-start = ((s16[16,144,128]{2,1,0:T(8,128)(2,1)}), s16[16,144,128]{2,1,0:T(8,128)(2,1)S(1)}, u32[]{:S(2)}, u32[]{:S(2)}) async-start(s16[16,144,128]{2,1,0:T(8,128)(2,1)} %get-tuple-element.7), calls=%async_computation | async-start | bytes 1179648 | tf_op jit(solution)/shard_map/all_to_all | solution.py:199
  12.0 18.6 %collective-permute-start = (s16[2,144,128]{2,1,0:T(8,128)(2,1)S(1)}, s16[2,144,128]{2,1,0:T(8,128)(2,1)S(1)}, u32[]{:S(2)}, u32[]{:S(2)}) collective-permute-start(s16[2,144,128]{2,1,0:T(8,128)(2,1)S(1)} %copy-done.4), channel_id=1, source_target_pairs={{0,17},{1,16},{2,19},{3,18},{4,21},{5,20},{6,23},{7,22},{8,25},{9,... | collective-permute-start | bytes 221192 | tf_op jit(solution)/shard_map/ppermute | solution.py:198
  24.6 13.8 %collective-permute-start.1 = (bf16[2,7,128,128]{3,2,1,0:T(8,128)(2,1)S(1)}, bf16[2,7,128,128]{3,2,1,0:T(8,128)(2,1)S(1)}, u32[]{:S(2)}, u32[]{:S(2)}) collective-permute-start(bf16[2,7,128,128]{3,2,1,0:T(8,128)(2,1)S(1)} %broadcast_select_fusion), channel_id=1, source_target_pairs={{0,128},{32,160},{64,192},{96,224},{128,0},{160,32},{192,64},{224,... | collective-permute-start | bytes 1376264 | tf_op jit(solution)/shard_map/ppermute | solution.py:197
  31.6 13.8 %copy-start.2 = (s32[64,7]{0,1:T(8,128)S(1)}, s32[64,7]{0,1:T(8,128)}, u32[]{:S(2)}) copy-start(s32[64,7]{0,1:T(8,128)} %param.6) | copy-start | bytes 5380
  31.6 13.8 %copy-start.3 = (s32[64]{0:T(128)S(1)}, s32[64]{0:T(128)}, u32[]{:S(2)}) copy-start(s32[64]{0:T(128)} %aggregates_ref.3) | copy-start | bytes 772
  31.6 13.8 %all-to-all-start.1 = ((s16[16,144,128]{2,1,0:T(8,128)(2,1)}), s16[16,144,128]{2,1,0:T(8,128)(2,1)S(1)}, u32[]{:S(2)}, u32[]{:S(2)}) async-start(s16[16,144,128]{2,1,0:T(8,128)(2,1)} %spread.1), calls=%async_computation.1 | async-start | bytes 1179648 | tf_op jit(solution)/shard_map/all_to_all | solution.py:209
  38.4 7.0 %collective-permute-start.2 = (bf16[2,7,128,128]{3,2,1,0:T(8,128)(2,1)S(1)}, bf16[2,7,128,128]{3,2,1,0:T(8,128)(2,1)S(1)}, u32[]{:S(2)}, u32[]{:S(2)}) collective-permute-start(bf16[2,7,128,128]{3,2,1,0:T(8,128)(2,1)S(1)} %collective-permute-done.1.a_or_p), channel_id=1, source_target_pairs={{0,2},{2,0},{4,6},{6,4},{8,10},{10,8},{12,14},{14,12},{16,18},{18,... | collective-permute-start | bytes 1376264 | tf_op jit(solution)/shard_map/ppermute | solution.py:210
